TPU v7x, 32 devices: a whole 2x2x4 slice. The times are simulated.
32 devices in a mesh: tile: 16 (over z, y, x), chan: 2 (over core).
Axes of the slice: x: 2, y: 2, z: 4, core: 2. Of those that a mesh axis runs over, the one named last changes fastest.
Arguments:
- panels: bfloat16 [64, 2, 256, 256], P('tile', 'chan'), may hold values from -6 to 6
- pair_ends: int32 [128, 2], P('tile'), may hold values from 0 to 63, as said below
- peaks: int32 [128, 8, 2], P(('tile', 'chan')), may hold values from 0 to 255
Outputs:
- surface: bfloat16 [128, 256, 256], P(('tile', 'chan'))
- scores: float32 [128, 8], P(('tile', 'chan'))
Inputs may be any that keep to these rules, and one draw needn't show every extreme that they name: `pair_ends`: rows p * 8 to (p + 1) * 8 - 1 belong to tile index p: their column 0 is a tile of that index's block of 4 tiles, column 1 another tile whose block is at most 2 indices away; distances 2 and -2 both occur.
All inputs are finite; a program needn't handle non-finite values.
Results may differ from a plain program's by a relative error of at most 0.017.
Values may be sent and summed in bfloat16 or wider, within the bound.
No kernel may reach another device: no remote copies, remote signals or barrier semaphores. Data moves between devices by JAX's collectives and lax.ppermute only.
A program may use at most 64 MiB of HBM per device.

v0:
```python
import functools
import math

import jax
import jax.numpy as jnp
import ml_dtypes
import numpy as np
from jax import lax
from jax.experimental import pallas as pl
from jax.experimental.pallas import tpu as pltpu
from jax.sharding import PartitionSpec as P

SIGMA = 0.5
FLOOR = 0.05
PLANE = 4
EXTRA = 8
BOTH = ("tile", "chan")
VMEM = pl.BlockSpec(memory_space=pltpu.VMEM)
SMEM = pl.BlockSpec(memory_space=pltpu.SMEM)
ANY = pl.BlockSpec(memory_space=pl.ANY)


def tables(size):
    index = np.arange(size)
    angle = (index[:, None] * index[None, :] % size) * (2.0 * math.pi / size)
    cosine = np.cos(angle).astype(ml_dtypes.bfloat16).astype(np.float64)
    sine = np.sin(angle).astype(ml_dtypes.bfloat16).astype(np.float64)
    offset = index[:, None] - index[None, :]
    weight = np.exp(-offset * offset / (2.0 * SIGMA * SIGMA))
    gauss = weight / weight.sum(axis=1, keepdims=True)
    half = size // 2
    columns = np.concatenate([cosine, -sine], axis=1)
    pad = np.zeros((EXTRA - 1, 2 * size))
    real = np.concatenate([cosine, sine], axis=1) / size
    imag = np.concatenate([-sine, cosine], axis=1) / size
    rows = np.concatenate([real[:half], imag[:half], real[half : half + 1], pad, imag[half : half + 1], pad], axis=0)
    back = np.block([[cosine, sine], [-sine, cosine]])
    twice = np.full((1, half), 2.0)
    twice[0, 0] = 1.0
    sines = -sine[:, :half] * twice
    sines[:, 0] = cosine[:, half]
    last = np.concatenate([cosine[:, :half] * twice, sines], axis=1) / size
    wide = np.concatenate([gauss.T, gauss], axis=1)
    narrow = np.concatenate([last, np.zeros((size, size))], axis=1)
    forward = np.concatenate([wide, columns, rows], axis=0)
    backward = np.concatenate([back, narrow], axis=0)
    return jnp.asarray(forward.astype(ml_dtypes.bfloat16)), jnp.asarray(backward.astype(ml_dtypes.bfloat16))


def product(left, right):
    return jnp.dot(left, right, preferred_element_type=jnp.float32)


def spectra_of(panels, table):
    count, size, _ = panels.shape
    first = product(panels.reshape(count * size, size), table[:size, :size]).astype(jnp.bfloat16)
    gauss = table[:size, size:]
    smooth = [product(gauss, first[k * size : (k + 1) * size]).astype(jnp.bfloat16) for k in range(count)]
    part = product(jnp.concatenate(smooth, axis=0), table[size : 2 * size]).astype(jnp.bfloat16)
    rows = table[2 * size :]
    slabs = []
    for k in range(count):
        one = part[k * size : (k + 1) * size]
        slabs.append(product(rows, jnp.concatenate([one[:, :size], one[:, size:]], axis=0)))
    return slabs


def spectra_kernel(core, *refs):
    panels, (table, out) = refs[:-2], refs[-2:]

    def work():
        for k, slab in enumerate(spectra_of(jnp.concatenate([p[...] for p in panels], axis=0), table)):
            out[k] = slab

    if core is None:
        work()
    else:
        pl.when(lax.axis_index("chan") == core)(work)


def split(slab, half):
    return (slab[:half], slab[half : 2 * half], slab[2 * half : 2 * half + EXTRA], slab[2 * half + EXTRA :])


def distances(here, chan):
    place = here % PLANE
    one = jnp.where(place % 2 == 0, 1, -1)
    two = jnp.where(place < 2, 2, -2)
    even = chan == 0
    never = 2 * PLANE
    return (
        0,
        jnp.where(even, two, one),
        jnp.where(even, one, two),
        jnp.where(even, -two, never),
        jnp.where(even, never, -two),
        -one,
    )


def cross_slab(a_slab, b_slab, half):
    a_real, a_imag, a_real_x, a_imag_x = split(a_slab, half)
    b_real, b_imag, b_real_x, b_imag_x = split(b_slab, half)
    parts = [
        a_real * b_real + a_imag * b_imag,
        a_imag * b_real - a_real * b_imag,
        a_real_x * b_real_x + a_imag_x * b_imag_x,
        a_imag_x * b_real_x - a_real_x * b_imag_x,
    ]
    return jnp.concatenate(parts, axis=0).astype(jnp.bfloat16)


def write_crosses(first_pair, cuts, ends, blocks, out, taken):
    here = lax.axis_index("tile")
    held = distances(here, lax.axis_index("chan"))
    own = blocks[0]
    tile_dev = own.shape[0]
    half = taken.shape[-1] // 2
    count = out.shape[0]
    for k in range(count):
        tile = ends[1, first_pair + k]
        away = tile // tile_dev - here
        slot = tile % tile_dev
        for (index, base), source in zip(cuts, blocks):
            size = source.shape[0]
            pick = away == held[index]
            if size < tile_dev:
                pick = pick & (slot >= base) & (slot < base + size)

            @pl.when(pick)
            def _(source=source, base=base):
                taken[k] = source[slot - base]

    for k in range(count):
        out[k] = cross_slab(own[ends[0, first_pair + k] - here * tile_dev], taken[k], half)


def cross_other_kernel(cuts, ends, *refs):
    blocks, (panels, table, out, slabs, taken, numbers, sem) = refs[: len(cuts) - 1], refs[len(cuts) - 1 :]
    copy = pltpu.make_async_copy(ends, numbers, sem)
    copy.start()
    for k, slab in enumerate(spectra_of(panels[...], table)):
        slabs[k] = slab
    copy.wait()
    first_pair = out.shape[0] * (1 - lax.axis_index("chan"))
    write_crosses(first_pair, cuts, numbers, (*blocks, slabs), out, taken)


def cross_mine_kernel(cuts, ends, *refs):
    blocks, (out, taken) = refs[: len(cuts)], refs[len(cuts) :]
    write_crosses(out.shape[0] * lax.axis_index("chan"), cuts, ends, blocks, out, taken)


def surface_kernel(spots, mine, other, table, surface, scores, corr, peaks, sem):
    copy = pltpu.make_async_copy(spots, peaks, sem)
    copy.start()
    count, _, size = surface.shape
    cand = scores.shape[1]
    half = size // 2
    parts = []
    for k in range(count):
        slab = mine[k].astype(jnp.float32) + other[k].astype(jnp.float32)
        real, imag, real_x, imag_x = split(slab, half)
        magnitude = jnp.sqrt(real * real + imag * imag)
        magnitude_x = jnp.sqrt(real_x * real_x + imag_x * imag_x)
        total = 2.0 * jnp.sum(magnitude) - jnp.sum(magnitude[:1]) + jnp.sum(magnitude_x)
        level = total / (size * size) + 1e-06
        scale = 1.0 / (magnitude + FLOOR * level)
        scale_x = 1.0 / (magnitude_x + FLOOR * level)
        q_real = jnp.concatenate([real * scale, real_x * scale_x], axis=0)
        q_imag = jnp.concatenate([imag * scale, imag_x * scale_x], axis=0)
        parts.append(jnp.concatenate([q_real, q_imag], axis=1))
    spread = half + EXTRA
    y_all = product(jnp.concatenate(parts, axis=0).astype(jnp.bfloat16), table[: 2 * size])
    last = table[2 * size :, :size]
    for k in range(count):
        y = y_all[k * spread : (k + 1) * spread]
        y_real = y[:half, :size]
        y_imag = y[:half, size:]
        row = lax.broadcasted_iota(jnp.int32, y_imag.shape, 0)
        y_imag = jnp.where(row == 0, y[half : half + 1, :size], y_imag)
        both = jnp.concatenate([y_real, y_imag], axis=0).astype(jnp.bfloat16)
        result = product(last, both)
        corr[k] = result
        surface[k] = result.astype(jnp.bfloat16)
    copy.wait()
    lane = lax.broadcasted_iota(jnp.int32, (1, size), 1)
    diagonal = lax.broadcasted_iota(jnp.int32, (cand, cand), 0) == lax.broadcasted_iota(jnp.int32, (cand, cand), 1)
    for k in range(count):
        picked = []
        for j in range(cand):
            row = corr[k, pl.ds(peaks[k, 0, j], 1), :]
            picked.append(jnp.where(lane == peaks[k, 1, j], row, 0.0))
        found = jnp.sum(jnp.concatenate(picked, axis=0), axis=1, keepdims=True)
        scores[k : k + 1, :] = jnp.sum(jnp.where(diagonal, found, 0.0), axis=0, keepdims=True)


def choose_kernel(first, second, out):
    place = lax.axis_index("tile") % PLANE
    outer = (place == 0) | (place == PLANE - 1)

    @pl.when(outer)
    def _():
        out[...] = first[...]

    @pl.when(jnp.logical_not(outer))
    def _():
        out[...] = second[...]


def routes(devices):
    def up(t, c):
        return (t + PLANE, c) if t + PLANE < devices else (t, 1 - c)

    def down(t, c):
        return (t - PLANE, c) if t >= PLANE else (t, 1 - c)

    def across(c, core):
        return 2 if c == core else 1

    def pairs(step):
        return [(2 * t + c, 2 * d + e) for t in range(devices) for c in range(2) for d, e in [step(t, c)]]

    return (
        pairs(lambda t, c: (t ^ across(c, 0), c)),
        pairs(lambda t, c: (t ^ across(c, 1), c)),
        pairs(lambda t, c: (up if (t % PLANE < 2) == (c == 0) else down)(t, c)),
        pairs(lambda t, c: (t ^ across(c, 1), c)),
        pairs(lambda t, c: (up if (t % PLANE < 2) == (c == 1) else down)(t, c)),
    )


def after(value, *earlier):
    return lax.optimization_barrier((value, *earlier))[0]


def call(kernel, name, operands, out, scratch=(), first=VMEM, flops=1 << 30):
    return pl.pallas_call(
        kernel,
        out_shape=out,
        in_specs=[first] + [VMEM] * (len(operands) - 1),
        out_specs=jax.tree.map(lambda _: VMEM, out),
        scratch_shapes=scratch,
        compiler_params=pltpu.CompilerParams(vmem_limit_bytes=8 << 20),
        cost_estimate=pl.CostEstimate(flops=flops, bytes_accessed=1 << 20, transcendentals=0),
        name=name,
    )(*operands)


def spectra_calls(table, slab, name, core, *panels):
    count, size = sum(p.shape[0] for p in panels), panels[0].shape[-1]
    return call(
        functools.partial(spectra_kernel, core),
        "spectra_" + name,
        (*panels, table),
        jax.ShapeDtypeStruct((count, slab, size), jnp.float32),
        flops=count * 12 * size**3,
    )


def chosen(first, second):
    return call(choose_kernel, "choose", (first, second), jax.ShapeDtypeStruct(first.shape, first.dtype), flops=1 << 20)


def shards(panels, pair_ends, peaks):
    tile_dev, _, size, _ = panels.shape
    share, cand, _ = peaks.shape
    devices = lax.axis_size("tile")
    local = panels[:, 0]
    forward, backward = tables(size)
    slab = size + 2 * EXTRA
    swap, cross_swap, climb, relay, climb_late = routes(devices)
    move = functools.partial(lax.ppermute, axis_name=BOTH)
    ends = pair_ends.T
    spots = jnp.transpose(peaks, (0, 2, 1))
    half = tile_dev // 2

    spectra = functools.partial(spectra_calls, forward, slab)
    parts = (local[:half], local[half:])
    got_swap = [move(part, perm=swap) for part in parts]
    own = spectra("own", None, *parts)
    got_cross = [move(after(part, got_swap[0]), perm=cross_swap) for part in parts]
    got_climb = [move(part, perm=climb) for part in got_swap]
    got_relay = [move(chosen(a, b), perm=relay) for a, b in zip(got_swap, got_climb)]
    got_late = [move(part, perm=climb_late) for part in got_cross]
    blocks = [
        own,
        spectra("swap", None, *got_swap),
        spectra("cross", None, *got_cross),
        spectra("climb", 0, *got_climb),
        spectra("late", 1, *got_late),
        spectra("relay", None, got_relay[0]),
    ]
    cuts = [(index, 0) for index in range(len(blocks))] + [(len(blocks) - 1, half)]
    crosses = jax.ShapeDtypeStruct((share, slab, size), jnp.bfloat16)
    taken = pltpu.VMEM((share, slab, size), jnp.float32)
    given, last = call(
        functools.partial(cross_other_kernel, cuts),
        "cross_other",
        (ends, *blocks, got_relay[1], forward),
        (crosses, jax.ShapeDtypeStruct((tile_dev - half, slab, size), jnp.float32)),
        [taken, pltpu.SMEM(ends.shape, ends.dtype), pltpu.SemaphoreType.DMA(())],
        ANY,
        flops=1 << 29,
    )
    other = lax.ppermute(given, "chan", [(0, 1), (1, 0)])
    kept = call(
        functools.partial(cross_mine_kernel, cuts),
        "cross_mine",
        (ends, *blocks, last),
        crosses,
        [taken],
        SMEM,
        flops=1 << 25,
    )
    return call(
        surface_kernel,
        "surface",
        (spots, kept, other, backward),
        (jax.ShapeDtypeStruct((share, size, size), jnp.bfloat16), jax.ShapeDtypeStruct((share, cand), jnp.float32)),
        [pltpu.VMEM((share, size, size), jnp.float32), pltpu.SMEM(spots.shape, spots.dtype), pltpu.SemaphoreType.DMA(())],
        ANY,
    )


def solution(mesh):
    in_specs = (P("tile", "chan", None, None), P("tile", None), P(BOTH, None, None))
    out_specs = (P(BOTH, None, None), P(BOTH, None))
    return jax.shard_map(shards, mesh=mesh, in_specs=in_specs, out_specs=out_specs, check_vma=False)
```

profile of v0, /device:TPU:0, one launch (start us, length us, event | category | flops | bytes accessed | tf_op | source)
XLA Modules:
  0.0 33.5 jit_solution(9162003380054011363)
XLA Ops:
  0.6 0.0 copy-start
  0.6 1.1 %slice_bitcast_fusion = (bf16[2,256,256]{2,1,0:T(8,128)(2,1)S(1)}, bf16[2,256,256]{2,1,0:T(8,128)(2,1)S(1)}) fusion(bf16[4,1,256,256]{3,2,0,1:T(8,128)(2,1)} %bitcast.10), kind=kLoop, calls=%fused_computation | loop fusion | bytes 1048576 | tf_op jit(solution)/shard_map/slice | solution.py:279
  1.8 3.0 %collective-permute-start = (bf16[2,256,256]{2,1,0:T(8,128)(2,1)S(1)}, bf16[2,256,256]{2,1,0:T(8,128)(2,1)S(1)}, u32[]{:S(2)}, u32[]{:S(2)}) collective-permute-start(bf16[2,256,256]{2,1,0:T(8,128)(2,1)S(1)} %get-tuple-element.6.refs_0_), channel_id=1, source_target_pairs={{0,4},{1,3},{2,6},{3,1},{4,0},{5,7},{6,2},{7,5},{8,12},{9,11},{10,... | collective-permute-start | bytes 786440 | tf_op jit(solution)/shard_map/ppermute | solution.py:280
  4.8 0.1 collective-permute-start.1
  4.9 4.3 %collective-permute-done.refs_0_.first = bf16[2,256,256]{2,1,0:T(8,128)(2,1)S(1)} collective-permute-done((bf16[2,256,256]{2,1,0:T(8,128)(2,1)S(1)}, bf16[2,256,256]{2,1,0:T(8,128)(2,1)S(1)}, u32[]{:S(2)}, u32[]{:S(2)}) %collective-permute-start) | collective-permute-done | bytes 262176 | tf_op jit(solution)/shard_map/ppermute | solution.py:280
  9.2 2.1 %collective-permute-start.4 = (bf16[2,256,256]{2,1,0:T(8,128)(2,1)S(1)}, bf16[2,256,256]{2,1,0:T(8,128)(2,1)S(1)}, u32[]{:S(2)}, u32[]{:S(2)}) collective-permute-start(bf16[2,256,256]{2,1,0:T(8,128)(2,1)S(1)} %collective-permute-done.refs_0_.first), channel_id=1, source_target_pairs={{0,8},{1,0},{2,10},{3,2},{4,5},{5,13},{6,7},{7,15},{8,16},{9,1},{1... | collective-permute-start | bytes 786440 | tf_op jit(solution)/shard_map/ppermute | solution.py:283
  11.2 1.5 %collective-permute-start.2 = (bf16[2,256,256]{2,1,0:T(8,128)(2,1)S(1)}, bf16[2,256,256]{2,1,0:T(8,128)(2,1)S(1)}, u32[]{:S(2)}, u32[]{:S(2)}) collective-permute-start(bf16[2,256,256]{2,1,0:T(8,128)(2,1)S(1)} %get-tuple-element.6.refs_0_), channel_id=1, source_target_pairs={{0,2},{1,5},{2,0},{3,7},{4,6},{5,1},{6,4},{7,3},{8,10},{9,13},{10,... | collective-permute-start | bytes 786440 | tf_op jit(solution)/shard_map/ppermute | solution.py:282
  12.7 0.5 %collective-permute-start.3 = (bf16[2,256,256]{2,1,0:T(8,128)(2,1)S(1)}, bf16[2,256,256]{2,1,0:T(8,128)(2,1)S(1)}, u32[]{:S(2)}, u32[]{:S(2)}) collective-permute-start(bf16[2,256,256]{2,1,0:T(8,128)(2,1)S(1)} %get-tuple-element.7.refs_1_), channel_id=1, source_target_pairs={{0,2},{1,5},{2,0},{3,7},{4,6},{5,1},{6,4},{7,3},{8,10},{9,13},{10,... | collective-permute-start | bytes 786440 | tf_op jit(solution)/shard_map/ppermute | solution.py:282
  13.3 0.0 collective-permute-done.1.refs_1_.first
  13.3 1.6 %collective-permute-start.5 = (bf16[2,256,256]{2,1,0:T(8,128)(2,1)S(1)}, bf16[2,256,256]{2,1,0:T(8,128)(2,1)S(1)}, u32[]{:S(2)}, u32[]{:S(2)}) collective-permute-start(bf16[2,256,256]{2,1,0:T(8,128)(2,1)S(1)} %collective-permute-done.1.refs_1_.first), channel_id=1, source_target_pairs={{0,8},{1,0},{2,10},{3,2},{4,5},{5,13},{6,7},{7,15},{8,16},{9,1},{1... | collective-permute-start | bytes 786440 | tf_op jit(solution)/shard_map/ppermute | solution.py:283
  14.9 0.3 collective-permute-done.4.refs_0_.second
  15.2 1.6 %collective-permute-start.8 = (bf16[2,256,256]{2,1,0:T(8,128)(2,1)S(1)}, bf16[2,256,256]{2,1,0:T(8,128)(2,1)S(1)}, u32[]{:S(2)}, u32[]{:S(2)}) collective-permute-start(bf16[2,256,256]{2,1,0:T(8,128)(2,1)S(1)} %choose.2), channel_id=1, source_target_pairs={{0,2},{1,5},{2,0},{3,7},{4,6},{5,1},{6,4},{7,3},{8,10},{9,13},{10,... | collective-permute-start | bytes 786440 | tf_op jit(solution)/shard_map/ppermute | solution.py:284
  16.7 0.0 copy-done
  16.7 1.2 %spectra_own.1.refs_0_ = f32[4,272,256]{2,1,0:T(8,128)S(1)} custom-call(bf16[2,256,256]{2,1,0:T(8,128)(2,1)S(1)} %get-tuple-element.6.refs_0_, bf16[2,256,256]{2,1,0:T(8,128)(2,1)S(1)} %get-tuple-element.7.refs_1_, bf16[784,512]{1,0:T(8,128)(2,1)S(1)} %copy-done), custom_call_target="tpu_custom_call" | custom-call | flops 805306368 | bytes 1048576 | tf_op jit(solution)/shard_map/spectra_own/pallas_call | solution.py:238
  17.9 0.0 collective-permute-done.2.refs_0_
  17.9 0.1 collective-permute-start.6
  18.0 2.5 %collective-permute-done.3.refs_1_ = bf16[2,256,256]{2,1,0:T(8,128)(2,1)S(1)} collective-permute-done((bf16[2,256,256]{2,1,0:T(8,128)(2,1)S(1)}, bf16[2,256,256]{2,1,0:T(8,128)(2,1)S(1)}, u32[]{:S(2)}, u32[]{:S(2)}) %collective-permute-start.3) | collective-permute-done | bytes 262176 | tf_op jit(solution)/shard_map/ppermute | solution.py:282
  20.4 0.0 collective-permute-start.7
  20.4 1.2 %spectra_swap.1.refs_1_ = f32[4,272,256]{2,1,0:T(8,128)S(1)} custom-call(bf16[2,256,256]{2,1,0:T(8,128)(2,1)S(1)} %collective-permute-done.refs_0_.first, bf16[2,256,256]{2,1,0:T(8,128)(2,1)S(1)} %collective-permute-done.1.refs_1_.first, bf16[784,512]{1,0:T(8,128)(2,1)S(1)} %copy-done), custom_call_target="tpu_custom_call" | custom-call | flops 805306368 | bytes 1048576 | tf_op jit(solution)/shard_map/spectra_swap/pallas_call | solution.py:238
  21.6 0.0 collective-permute-done.5.refs_1_.second
  21.7 1.6 %collective-permute-start.9 = (bf16[2,256,256]{2,1,0:T(8,128)(2,1)S(1)}, bf16[2,256,256]{2,1,0:T(8,128)(2,1)S(1)}, u32[]{:S(2)}, u32[]{:S(2)}) collective-permute-start(bf16[2,256,256]{2,1,0:T(8,128)(2,1)S(1)} %choose.3), channel_id=1, source_target_pairs={{0,2},{1,5},{2,0},{3,7},{4,6},{5,1},{6,4},{7,3},{8,10},{9,13},{10,... | collective-permute-start | bytes 786440 | tf_op jit(solution)/shard_map/ppermute | solution.py:284
  23.2 1.2 %spectra_climb.1.refs_3_ = f32[4,272,256]{2,1,0:T(8,128)S(1)} custom-call(bf16[2,256,256]{2,1,0:T(8,128)(2,1)S(1)} %collective-permute-done.4.refs_0_.second, bf16[2,256,256]{2,1,0:T(8,128)(2,1)S(1)} %collective-permute-done.5.refs_1_.second, bf16[784,512]{1,0:T(8,128)(2,1)S(1)} %copy-done), custom_call_target="tpu_custom_call" | custom-call | flops 805306368 | bytes 1048576 | tf_op jit(solution)/shard_map/spectra_climb/pallas_call | solution.py:238
  24.4 1.2 %spectra_cross.1.refs_2_ = f32[4,272,256]{2,1,0:T(8,128)S(1)} custom-call(bf16[2,256,256]{2,1,0:T(8,128)(2,1)S(1)} %collective-permute-done.2.refs_0_, bf16[2,256,256]{2,1,0:T(8,128)(2,1)S(1)} %collective-permute-done.3.refs_1_, bf16[784,512]{1,0:T(8,128)(2,1)S(1)} %copy-done), custom_call_target="tpu_custom_call" | custom-call | flops 805306368 | bytes 1048576 | tf_op jit(solution)/shard_map/spectra_cross/pallas_call | solution.py:238
  25.6 0.0 collective-permute-done.8.refs_0_
  25.6 0.8 %spectra_relay.1.refs_5_ = f32[2,272,256]{2,1,0:T(8,128)S(1)} custom-call(bf16[2,256,256]{2,1,0:T(8,128)(2,1)S(1)} %collective-permute-done.8.refs_0_, bf16[784,512]{1,0:T(8,128)(2,1)S(1)} %copy-done), custom_call_target="tpu_custom_call" | custom-call | flops 402653184 | bytes 1048576 | tf_op jit(solution)/shard_map/spectra_relay/pallas_call | solution.py:238
  26.4 0.0 copy-start.1
  26.4 0.0 collective-permute-done.6.refs_0_
  26.4 1.2 %collective-permute-done.7.refs_1_ = bf16[2,256,256]{2,1,0:T(8,128)(2,1)S(1)} collective-permute-done((bf16[2,256,256]{2,1,0:T(8,128)(2,1)S(1)}, bf16[2,256,256]{2,1,0:T(8,128)(2,1)S(1)}, u32[]{:S(2)}, u32[]{:S(2)}) %collective-permute-start.7) | collective-permute-done | bytes 262176 | tf_op jit(solution)/shard_map/ppermute | solution.py:285
  27.6 0.5 %collective-permute-done.9.refs_6_ = bf16[2,256,256]{2,1,0:T(8,128)(2,1)S(1)} collective-permute-done((bf16[2,256,256]{2,1,0:T(8,128)(2,1)S(1)}, bf16[2,256,256]{2,1,0:T(8,128)(2,1)S(1)}, u32[]{:S(2)}, u32[]{:S(2)}) %collective-permute-start.9) | collective-permute-done | bytes 262176 | tf_op jit(solution)/shard_map/ppermute | solution.py:284
  28.1 0.0 copy-done.1
  28.1 1.4 %cross_other.1 = (bf16[4,272,256]{2,1,0:T(8,128)(2,1)S(1)}, f32[2,272,256]{2,1,0:T(8,128)S(1)}) custom-call(s32[2,8]{1,0:T(2,128)S(1)} %bitcast.7, f32[4,272,256]{2,1,0:T(8,128)S(1)} %spectra_own.1.refs_0_, f32[4,272,256]{2,1,0:T(8,128)S(1)} %spectra_swap.1.refs_1_, f32[4,272,256]{2,1,0:T(8,128)S(1)} %spectra_cross.1.refs_2_, ...), custom_call_target="tpu_custom_call" | custom-call | flops 536870912 | bytes 1048576 | tf_op jit(solution)/shard_map/cross_other/pallas_call | solution.py:238
  29.5 0.1 collective-permute-start.10
  29.5 0.0 copy-start.2
  29.6 0.0 copy-start.3
  29.6 1.0 %cross_mine.1.mine = bf16[4,272,256]{2,1,0:T(8,128)(2,1)S(1)} custom-call(s32[2,8]{1,0:T(2,128)S(1)} %bitcast.8, f32[4,272,256]{2,1,0:T(8,128)S(1)} %spectra_own.1.refs_0_, f32[4,272,256]{2,1,0:T(8,128)S(1)} %spectra_swap.1.refs_1_, f32[4,272,256]{2,1,0:T(8,128)S(1)} %spectra_cross.1.refs_2_, f32[4,272,256]{2,1,0:T(8,128)S(1)} %spectra_climb.1.refs_3_, ...), custom_call_target="tpu_custom_call" | custom-call | flops 33554432 | bytes 1048576 | tf_op jit(solution)/shard_map/cross_mine/pallas_call | solution.py:238
  30.6 0.9 %collective-permute-done.10.other = bf16[4,272,256]{2,1,0:T(8,128)(2,1)S(1)} collective-permute-done((bf16[4,272,256]{2,1,0:T(8,128)(2,1)S(1)}, bf16[4,272,256]{2,1,0:T(8,128)(2,1)S(1)}, u32[]{:S(2)}, u32[]{:S(2)}) %collective-permute-start.10) | collective-permute-done | bytes 557088 | tf_op jit(solution)/shard_map/ppermute | solution.py:306
  31.5 0.0 copy-done.2
  31.5 0.0 copy-done.3
  31.5 2.0 %surface.1 = (bf16[4,256,256]{2,1,0:T(8,128)(2,1)}, f32[4,8]{1,0:T(4,128)}) custom-call(s32[4,2,8]{2,1,0:T(2,128)S(1)} %bitcast.9, bf16[4,272,256]{2,1,0:T(8,128)(2,1)S(1)} %cross_mine.1.mine, bf16[4,272,256]{2,1,0:T(8,128)(2,1)S(1)} %collective-permute-done.10.other, bf16[768,512]{1,0:T(8,128)(2,1)S(1)} %copy-done.3), custom_call_target="tpu_custom_call" | custom-call | flops 1073741824 | bytes 1048576 | tf_op jit(solution)/shard_map/surface/pallas_call | solution.py:238
  (3 shorter events, 0.1 us)
Async XLA Ops:
  0.6 16.1 %copy-start = (bf16[784,512]{1,0:T(8,128)(2,1)S(1)}, bf16[784,512]{1,0:T(8,128)(2,1)}, u32[]{:S(2)}) copy-start(bf16[784,512]{1,0:T(8,128)(2,1)} %constant.4.clone.refs_2_.refs_1_.refs_7_) | copy-start | bytes 2408452
  1.8 7.4 %collective-permute-start = (bf16[2,256,256]{2,1,0:T(8,128)(2,1)S(1)}, bf16[2,256,256]{2,1,0:T(8,128)(2,1)S(1)}, u32[]{:S(2)}, u32[]{:S(2)}) collective-permute-start(bf16[2,256,256]{2,1,0:T(8,128)(2,1)S(1)} %get-tuple-element.6.refs_0_), channel_id=1, source_target_pairs={{0,4},{1,3},{2,6},{3,1},{4,0},{5,7},{6,2},{7,5},{8,12},{9,11},{10,... | collective-permute-start | bytes 786440 | tf_op jit(solution)/shard_map/ppermute | solution.py:280
  4.8 8.5 %collective-permute-start.1 = (bf16[2,256,256]{2,1,0:T(8,128)(2,1)S(1)}, bf16[2,256,256]{2,1,0:T(8,128)(2,1)S(1)}, u32[]{:S(2)}, u32[]{:S(2)}) collective-permute-start(bf16[2,256,256]{2,1,0:T(8,128)(2,1)S(1)} %get-tuple-element.7.refs_1_), channel_id=1, source_target_pairs={{0,4},{1,3},{2,6},{3,1},{4,0},{5,7},{6,2},{7,5},{8,12},{9,11},{10,... | collective-permute-start | bytes 786440 | tf_op jit(solution)/shard_map/ppermute | solution.py:280
  9.2 6.0 %collective-permute-start.4 = (bf16[2,256,256]{2,1,0:T(8,128)(2,1)S(1)}, bf16[2,256,256]{2,1,0:T(8,128)(2,1)S(1)}, u32[]{:S(2)}, u32[]{:S(2)}) collective-permute-start(bf16[2,256,256]{2,1,0:T(8,128)(2,1)S(1)} %collective-permute-done.refs_0_.first), channel_id=1, source_target_pairs={{0,8},{1,0},{2,10},{3,2},{4,5},{5,13},{6,7},{7,15},{8,16},{9,1},{1... | collective-permute-start | bytes 786440 | tf_op jit(solution)/shard_map/ppermute | solution.py:283
  11.2 6.6 %collective-permute-start.2 = (bf16[2,256,256]{2,1,0:T(8,128)(2,1)S(1)}, bf16[2,256,256]{2,1,0:T(8,128)(2,1)S(1)}, u32[]{:S(2)}, u32[]{:S(2)}) collective-permute-start(bf16[2,256,256]{2,1,0:T(8,128)(2,1)S(1)} %get-tuple-element.6.refs_0_), channel_id=1, source_target_pairs={{0,2},{1,5},{2,0},{3,7},{4,6},{5,1},{6,4},{7,3},{8,10},{9,13},{10,... | collective-permute-start | bytes 786440 | tf_op jit(solution)/shard_map/ppermute | solution.py:282
  12.7 7.7 %collective-permute-start.3 = (bf16[2,256,256]{2,1,0:T(8,128)(2,1)S(1)}, bf16[2,256,256]{2,1,0:T(8,128)(2,1)S(1)}, u32[]{:S(2)}, u32[]{:S(2)}) collective-permute-start(bf16[2,256,256]{2,1,0:T(8,128)(2,1)S(1)} %get-tuple-element.7.refs_1_), channel_id=1, source_target_pairs={{0,2},{1,5},{2,0},{3,7},{4,6},{5,1},{6,4},{7,3},{8,10},{9,13},{10,... | collective-permute-start | bytes 786440 | tf_op jit(solution)/shard_map/ppermute | solution.py:282
  13.3 8.3 %collective-permute-start.5 = (bf16[2,256,256]{2,1,0:T(8,128)(2,1)S(1)}, bf16[2,256,256]{2,1,0:T(8,128)(2,1)S(1)}, u32[]{:S(2)}, u32[]{:S(2)}) collective-permute-start(bf16[2,256,256]{2,1,0:T(8,128)(2,1)S(1)} %collective-permute-done.1.refs_1_.first), channel_id=1, source_target_pairs={{0,8},{1,0},{2,10},{3,2},{4,5},{5,13},{6,7},{7,15},{8,16},{9,1},{1... | collective-permute-start | bytes 786440 | tf_op jit(solution)/shard_map/ppermute | solution.py:283
  15.2 10.4 %collective-permute-start.8 = (bf16[2,256,256]{2,1,0:T(8,128)(2,1)S(1)}, bf16[2,256,256]{2,1,0:T(8,128)(2,1)S(1)}, u32[]{:S(2)}, u32[]{:S(2)}) collective-permute-start(bf16[2,256,256]{2,1,0:T(8,128)(2,1)S(1)} %choose.2), channel_id=1, source_target_pairs={{0,2},{1,5},{2,0},{3,7},{4,6},{5,1},{6,4},{7,3},{8,10},{9,13},{10,... | collective-permute-start | bytes 786440 | tf_op jit(solution)/shard_map/ppermute | solution.py:284
  17.9 8.5 %collective-permute-start.6 = (bf16[2,256,256]{2,1,0:T(8,128)(2,1)S(1)}, bf16[2,256,256]{2,1,0:T(8,128)(2,1)S(1)}, u32[]{:S(2)}, u32[]{:S(2)}) collective-permute-start(bf16[2,256,256]{2,1,0:T(8,128)(2,1)S(1)} %collective-permute-done.2.refs_0_), channel_id=1, source_target_pairs={{0,1},{1,9},{2,3},{3,11},{4,12},{5,4},{6,14},{7,6},{8,0},{9,17},{1... | collective-permute-start | bytes 786440 | tf_op jit(solution)/shard_map/ppermute | solution.py:285
  20.4 7.2 %collective-permute-start.7 = (bf16[2,256,256]{2,1,0:T(8,128)(2,1)S(1)}, bf16[2,256,256]{2,1,0:T(8,128)(2,1)S(1)}, u32[]{:S(2)}, u32[]{:S(2)}) collective-permute-start(bf16[2,256,256]{2,1,0:T(8,128)(2,1)S(1)} %collective-permute-done.3.refs_1_), channel_id=1, source_target_pairs={{0,1},{1,9},{2,3},{3,11},{4,12},{5,4},{6,14},{7,6},{8,0},{9,17},{1... | collective-permute-start | bytes 786440 | tf_op jit(solution)/shard_map/ppermute | solution.py:285
  21.7 6.4 %collective-permute-start.9 = (bf16[2,256,256]{2,1,0:T(8,128)(2,1)S(1)}, bf16[2,256,256]{2,1,0:T(8,128)(2,1)S(1)}, u32[]{:S(2)}, u32[]{:S(2)}) collective-permute-start(bf16[2,256,256]{2,1,0:T(8,128)(2,1)S(1)} %choose.3), channel_id=1, source_target_pairs={{0,2},{1,5},{2,0},{3,7},{4,6},{5,1},{6,4},{7,3},{8,10},{9,13},{10,... | collective-permute-start | bytes 786440 | tf_op jit(solution)/shard_map/ppermute | solution.py:284
  26.4 1.7 %copy-start.1 = (s32[8,2]{0,1:T(2,128)S(1)}, s32[8,2]{0,1:T(2,128)}, u32[]{:S(2)}) copy-start(s32[8,2]{0,1:T(2,128)} %param.6) | copy-start | bytes 196
  29.5 2.0 %collective-permute-start.10 = (bf16[4,272,256]{2,1,0:T(8,128)(2,1)S(1)}, bf16[4,272,256]{2,1,0:T(8,128)(2,1)S(1)}, u32[]{:S(2)}, u32[]{:S(2)}) collective-permute-start(bf16[4,272,256]{2,1,0:T(8,128)(2,1)S(1)} %get-tuple-element.9), channel_id=1, source_target_pairs={{0,1},{1,0},{2,3},{3,2},{4,5},{5,4},{6,7},{7,6},{8,9},{9,8},{10,11... | collective-permute-start | bytes 1671176 | tf_op jit(solution)/shard_map/ppermute | solution.py:306
  29.5 1.9 %copy-start.2 = (s32[4,8,2]{1,2,0:T(2,128)S(1)}, s32[4,8,2]{1,2,0:T(2,128)}, u32[]{:S(2)}) copy-start(s32[4,8,2]{1,2,0:T(2,128)} %param.7) | copy-start | bytes 772
  29.6 1.9 %copy-start.3 = (bf16[768,512]{1,0:T(8,128)(2,1)S(1)}, bf16[768,512]{1,0:T(8,128)(2,1)}, u32[]{:S(2)}) copy-start(bf16[768,512]{1,0:T(8,128)(2,1)} %constant.5.clone.table) | copy-start | bytes 2359300
where the time goes:
time: 34 us; the launch traced here: 33.5 us
  starting transfers between devices  12 us (35%)
  Pallas kernels  9.91 us (29%)
  waiting for transfers between devices  9.56 us (28%)
  local copies, waits for them, and re-layouts  1.16 us (3%)
  between operations  0.78 us (2%)
    pallas_call x11, Pallas kernels, call(): pl.pallas_call(kernel, out_shape=out, in_specs=[first] + [VMEM] * (len(op...  9.91 us
    ppermute x2, waiting for transfers between devices, shards(): got_swap = [move(part, perm=swap) for part in parts]  4.28 us
    ppermute x2, starting transfers between devices, shards(): got_climb = [move(part, perm=climb) for part in got_swap]  3.65 us
    ppermute x2, starting transfers between devices, shards(): got_swap = [move(part, perm=swap) for part in parts]  3.11 us
    ppermute x2, starting transfers between devices, shards(): move(chosen(a, b), perm=relay)  3.11 us
    ppermute x2, waiting for transfers between devices, shards(): move(after(part, got_swap[0]), perm=cross_swap)  2.46 us
    ppermute x2, starting transfers between devices, shards(): move(after(part, got_swap[0]), perm=cross_swap)  2.03 us
    ppermute x2, waiting for transfers between devices, shards(): got_late = [move(part, perm=climb_late) for part in got_cross]  1.16 us
  transfers between devices with their start and end apart: 11, of which 6 were waited for; matrix products, arithmetic and copies ran while one was open for 0% of the time, Pallas kernels for 20%

commit v1 on v0

--- a/solution.py
+++ b/solution.py
@@ -247,19 +247,19 @@
     )(*operands)
 
 
-def spectra_calls(table, slab, name, core, *panels):
+def spectra_calls(table, slab, name, core, *panels, flops=None):
     count, size = sum(p.shape[0] for p in panels), panels[0].shape[-1]
     return call(
         functools.partial(spectra_kernel, core),
         "spectra_" + name,
         (*panels, table),
         jax.ShapeDtypeStruct((count, slab, size), jnp.float32),
-        flops=count * 12 * size**3,
-    )
-
-
-def chosen(first, second):
-    return call(choose_kernel, "choose", (first, second), jax.ShapeDtypeStruct(first.shape, first.dtype), flops=1 << 20)
+        flops=flops or count * 12 * size**3,
+    )
+
+
+def chosen(first, second, flops):
+    return call(choose_kernel, "choose", (first, second), jax.ShapeDtypeStruct(first.shape, first.dtype), flops=flops)
 
 
 def shards(panels, pair_ends, peaks):
@@ -279,18 +279,17 @@
     parts = (local[:half], local[half:])
     got_swap = [move(part, perm=swap) for part in parts]
     own = spectra("own", None, *parts)
-    got_cross = [move(after(part, got_swap[0]), perm=cross_swap) for part in parts]
+    got_cross = [move(after(part, got_swap[0], own), perm=cross_swap) for part in parts]
     got_climb = [move(part, perm=climb) for part in got_swap]
-    got_relay = [move(chosen(a, b), perm=relay) for a, b in zip(got_swap, got_climb)]
+    picked = [chosen(a, b, flops) for a, b, flops in zip(got_swap, got_climb, (1 << 20, 3_000_000_000))]
+    got_relay = [move(part, perm=relay) for part in picked]
     got_late = [move(part, perm=climb_late) for part in got_cross]
-    blocks = [
-        own,
-        spectra("swap", None, *got_swap),
-        spectra("cross", None, *got_cross),
-        spectra("climb", 0, *got_climb),
-        spectra("late", 1, *got_late),
-        spectra("relay", None, got_relay[0]),
-    ]
+    from_swap = spectra("swap", None, after(got_swap[0], got_relay[0]), got_swap[1])
+    from_cross = spectra("cross", None, *got_cross, flops=1_000_000)
+    from_climb = spectra("climb", 0, after(got_climb[0], from_swap), got_climb[1], flops=1_000_000)
+    from_relay = spectra("relay", None, got_relay[0], flops=800_000_000)
+    from_late = spectra("late", 1, *got_late)
+    blocks = [own, from_swap, from_cross, from_climb, from_late, from_relay]
     cuts = [(index, 0) for index in range(len(blocks))] + [(len(blocks) - 1, half)]
     crosses = jax.ShapeDtypeStruct((share, slab, size), jnp.bfloat16)
     taken = pltpu.VMEM((share, slab, size), jnp.float32)

time: 34 us -> 32.6 us (0.959); the launches traced: 33.5 us -> 32.4 us
  waiting for transfers between devices: 9.56 us -> 7.31 us
  local copies, waits for them, and re-layouts: 1.16 us -> 2.45 us
    ppermute x2, waiting for transfers between devices: 4.28 us -> 1.97 us  [shards(): got_swap = [move(part, perm=swap) for part in parts]]
    unnamed x8 -> x10, local copies, waits for them, and re-layouts: 0.03 us -> 1.39 us
    ppermute x4, waiting for transfers between devices: 2.96 us -> 3.84 us  [the longest x2 3.7 us: shards(): move(after(part, got_swap[0], own), perm=cross_swap)]
    ppermute x2, waiting for transfers between devices: 1.16 us -> 0.34 us  [shards(): got_late = [move(part, perm=climb_late) for part in got_cross]]
  transfers between devices with their start and end apart: 11 -> 11, of which waited for: 6 -> 7; matrix products, arithmetic and copies ran while one was open for 0% -> 0% of each run, Pallas kernels for 20% -> 20%
where the time goes in v1:
time: 32.6 us; the launch traced here: 32.4 us
  starting transfers between devices  12 us (37%)
  Pallas kernels  9.93 us (30%)
  waiting for transfers between devices  7.31 us (22%)
  local copies, waits for them, and re-layouts  2.45 us (8%)
  between operations  0.75 us (2%)
    pallas_call x11, Pallas kernels, call(): pl.pallas_call(kernel, out_shape=out, in_specs=[first] + [VMEM] * (len(op...  9.93 us
    ppermute x2, waiting for transfers between devices, shards(): move(after(part, got_swap[0], own), perm=cross_swap)  3.7 us
    ppermute x2, starting transfers between devices, shards(): got_climb = [move(part, perm=climb) for part in got_swap]  3.65 us
    ppermute x2, starting transfers between devices, shards(): got_swap = [move(part, perm=swap) for part in parts]  3.11 us
    ppermute x2, starting transfers between devices, shards(): got_relay = [move(part, perm=relay) for part in picked]  3.11 us
    ppermute x2, starting transfers between devices, shards(): move(after(part, got_swap[0], own), perm=cross_swap)  2.03 us
    ppermute x2, waiting for transfers between devices, shards(): got_swap = [move(part, perm=swap) for part in parts]  1.97 us
    unnamed x10, local copies, waits for them, and re-layouts  1.39 us
  transfers between devices with their start and end apart: 11, of which 7 were waited for; matrix products, arithmetic and copies ran while one was open for 0% of the time, Pallas kernels for 20%

profile of v1, /device:TPU:0, one launch (start us, length us, event | category | flops | bytes accessed | tf_op | source)
XLA Modules:
  0.0 32.4 jit_solution(5061968250693185713)
XLA Ops:
  0.6 1.1 %slice_bitcast_fusion = (bf16[2,256,256]{2,1,0:T(8,128)(2,1)S(1)}, bf16[2,256,256]{2,1,0:T(8,128)(2,1)S(1)}) fusion(bf16[4,1,256,256]{3,2,0,1:T(8,128)(2,1)} %bitcast.10), kind=kLoop, calls=%fused_computation | loop fusion | bytes 1048576 | tf_op jit(solution)/shard_map/slice | solution.py:279
  1.7 3.0 %collective-permute-start = (bf16[2,256,256]{2,1,0:T(8,128)(2,1)S(1)}, bf16[2,256,256]{2,1,0:T(8,128)(2,1)S(1)}, u32[]{:S(2)}, u32[]{:S(2)}) collective-permute-start(bf16[2,256,256]{2,1,0:T(8,128)(2,1)S(1)} %get-tuple-element.9.refs_0_), channel_id=1, source_target_pairs={{0,4},{1,3},{2,6},{3,1},{4,0},{5,7},{6,2},{7,5},{8,12},{9,11},{10,... | collective-permute-start | bytes 786440 | tf_op jit(solution)/shard_map/ppermute | solution.py:280
  4.7 0.1 collective-permute-start.3
  4.8 0.0 copy-start
  4.8 1.1 %copy-done = bf16[784,512]{1,0:T(8,128)(2,1)S(1)} copy-done((bf16[784,512]{1,0:T(8,128)(2,1)S(1)}, bf16[784,512]{1,0:T(8,128)(2,1)}, u32[]{:S(2)}) %copy-start) | copy-done | bytes 802840
  5.9 1.2 %spectra_own.1.refs_0_ = f32[4,272,256]{2,1,0:T(8,128)S(1)} custom-call(bf16[2,256,256]{2,1,0:T(8,128)(2,1)S(1)} %get-tuple-element.9.refs_0_, bf16[2,256,256]{2,1,0:T(8,128)(2,1)S(1)} %get-tuple-element.10.refs_1_, bf16[784,512]{1,0:T(8,128)(2,1)S(1)} %copy-done), custom_call_target="tpu_custom_call" | custom-call | flops 805306368 | bytes 1048576 | tf_op jit(solution)/shard_map/spectra_own/pallas_call | solution.py:238
  7.1 2.0 %collective-permute-done.first.refs_0_ = bf16[2,256,256]{2,1,0:T(8,128)(2,1)S(1)} collective-permute-done((bf16[2,256,256]{2,1,0:T(8,128)(2,1)S(1)}, bf16[2,256,256]{2,1,0:T(8,128)(2,1)S(1)}, u32[]{:S(2)}, u32[]{:S(2)}) %collective-permute-start) | collective-permute-done | bytes 262176 | tf_op jit(solution)/shard_map/ppermute | solution.py:280
  9.1 2.1 %collective-permute-start.1 = (bf16[2,256,256]{2,1,0:T(8,128)(2,1)S(1)}, bf16[2,256,256]{2,1,0:T(8,128)(2,1)S(1)}, u32[]{:S(2)}, u32[]{:S(2)}) collective-permute-start(bf16[2,256,256]{2,1,0:T(8,128)(2,1)S(1)} %collective-permute-done.first.refs_0_), channel_id=1, source_target_pairs={{0,8},{1,0},{2,10},{3,2},{4,5},{5,13},{6,7},{7,15},{8,16},{9,1},{1... | collective-permute-start | bytes 786440 | tf_op jit(solution)/shard_map/ppermute | solution.py:283
  11.2 1.5 %collective-permute-start.4 = (bf16[2,256,256]{2,1,0:T(8,128)(2,1)S(1)}, bf16[2,256,256]{2,1,0:T(8,128)(2,1)S(1)}, u32[]{:S(2)}, u32[]{:S(2)}) collective-permute-start(bf16[2,256,256]{2,1,0:T(8,128)(2,1)S(1)} %get-tuple-element.9.refs_0_), channel_id=1, source_target_pairs={{0,2},{1,5},{2,0},{3,7},{4,6},{5,1},{6,4},{7,3},{8,10},{9,13},{10,... | collective-permute-start | bytes 786440 | tf_op jit(solution)/shard_map/ppermute | solution.py:282
  12.7 0.5 %collective-permute-start.5 = (bf16[2,256,256]{2,1,0:T(8,128)(2,1)S(1)}, bf16[2,256,256]{2,1,0:T(8,128)(2,1)S(1)}, u32[]{:S(2)}, u32[]{:S(2)}) collective-permute-start(bf16[2,256,256]{2,1,0:T(8,128)(2,1)S(1)} %get-tuple-element.10.refs_1_), channel_id=1, source_target_pairs={{0,2},{1,5},{2,0},{3,7},{4,6},{5,1},{6,4},{7,3},{8,10},{9,13},{10,... | collective-permute-start | bytes 786440 | tf_op jit(solution)/shard_map/ppermute | solution.py:282
  13.2 0.0 collective-permute-done.3.refs_1_.first
  13.2 1.6 %collective-permute-start.6 = (bf16[2,256,256]{2,1,0:T(8,128)(2,1)S(1)}, bf16[2,256,256]{2,1,0:T(8,128)(2,1)S(1)}, u32[]{:S(2)}, u32[]{:S(2)}) collective-permute-start(bf16[2,256,256]{2,1,0:T(8,128)(2,1)S(1)} %collective-permute-done.3.refs_1_.first), channel_id=1, source_target_pairs={{0,8},{1,0},{2,10},{3,2},{4,5},{5,13},{6,7},{7,15},{8,16},{9,1},{1... | collective-permute-start | bytes 786440 | tf_op jit(solution)/shard_map/ppermute | solution.py:283
  14.8 0.3 collective-permute-done.1.second.refs_0_
  15.1 0.0 copy-start.1
  15.1 1.6 %collective-permute-start.2 = (bf16[2,256,256]{2,1,0:T(8,128)(2,1)S(1)}, bf16[2,256,256]{2,1,0:T(8,128)(2,1)S(1)}, u32[]{:S(2)}, u32[]{:S(2)}) collective-permute-start(bf16[2,256,256]{2,1,0:T(8,128)(2,1)S(1)} %choose.2), channel_id=1, source_target_pairs={{0,2},{1,5},{2,0},{3,7},{4,6},{5,1},{6,4},{7,3},{8,10},{9,13},{10,... | collective-permute-start | bytes 786440 | tf_op jit(solution)/shard_map/ppermute | solution.py:285
  16.6 0.9 %collective-permute-done.4.refs_0_ = bf16[2,256,256]{2,1,0:T(8,128)(2,1)S(1)} collective-permute-done((bf16[2,256,256]{2,1,0:T(8,128)(2,1)S(1)}, bf16[2,256,256]{2,1,0:T(8,128)(2,1)S(1)}, u32[]{:S(2)}, u32[]{:S(2)}) %collective-permute-start.4) | collective-permute-done | bytes 262176 | tf_op jit(solution)/shard_map/ppermute | solution.py:282
  17.5 0.0 collective-permute-start.7
  17.5 2.8 %collective-permute-done.5.refs_1_ = bf16[2,256,256]{2,1,0:T(8,128)(2,1)S(1)} collective-permute-done((bf16[2,256,256]{2,1,0:T(8,128)(2,1)S(1)}, bf16[2,256,256]{2,1,0:T(8,128)(2,1)S(1)}, u32[]{:S(2)}, u32[]{:S(2)}) %collective-permute-start.5) | collective-permute-done | bytes 262176 | tf_op jit(solution)/shard_map/ppermute | solution.py:282
  20.3 0.0 collective-permute-start.8
  20.3 0.0 collective-permute-done.6.refs_1_.second
  20.4 1.6 %collective-permute-start.9 = (bf16[2,256,256]{2,1,0:T(8,128)(2,1)S(1)}, bf16[2,256,256]{2,1,0:T(8,128)(2,1)S(1)}, u32[]{:S(2)}, u32[]{:S(2)}) collective-permute-start(bf16[2,256,256]{2,1,0:T(8,128)(2,1)S(1)} %choose.3), channel_id=1, source_target_pairs={{0,2},{1,5},{2,0},{3,7},{4,6},{5,1},{6,4},{7,3},{8,10},{9,13},{10,... | collective-permute-start | bytes 786440 | tf_op jit(solution)/shard_map/ppermute | solution.py:285
  21.9 0.0 copy-done.1
  21.9 1.2 %spectra_cross.1.refs_2_ = f32[4,272,256]{2,1,0:T(8,128)S(1)} custom-call(bf16[2,256,256]{2,1,0:T(8,128)(2,1)S(1)} %collective-permute-done.4.refs_0_, bf16[2,256,256]{2,1,0:T(8,128)(2,1)S(1)} %collective-permute-done.5.refs_1_, bf16[784,512]{1,0:T(8,128)(2,1)S(1)} %copy-done.1), custom_call_target="tpu_custom_call" | custom-call | flops 1000000 | bytes 1048576 | tf_op jit(solution)/shard_map/spectra_cross/pallas_call | solution.py:238
  23.1 0.0 collective-permute-done.2.refs_0_
  23.1 1.2 %spectra_swap.1.refs_1_ = f32[4,272,256]{2,1,0:T(8,128)S(1)} custom-call(bf16[2,256,256]{2,1,0:T(8,128)(2,1)S(1)} %collective-permute-done.first.refs_0_, bf16[2,256,256]{2,1,0:T(8,128)(2,1)S(1)} %collective-permute-done.3.refs_1_.first, bf16[784,512]{1,0:T(8,128)(2,1)S(1)} %copy-done.1), custom_call_target="tpu_custom_call" | custom-call | flops 805306368 | bytes 1048576 | tf_op jit(solution)/shard_map/spectra_swap/pallas_call | solution.py:238
  24.3 1.2 %spectra_climb.1.refs_3_ = f32[4,272,256]{2,1,0:T(8,128)S(1)} custom-call(bf16[2,256,256]{2,1,0:T(8,128)(2,1)S(1)} %collective-permute-done.1.second.refs_0_, bf16[2,256,256]{2,1,0:T(8,128)(2,1)S(1)} %collective-permute-done.6.refs_1_.second, bf16[784,512]{1,0:T(8,128)(2,1)S(1)} %copy-done.1), custom_call_target="tpu_custom_call" | custom-call | flops 1000000 | bytes 1048576 | tf_op jit(solution)/shard_map/spectra_climb/pallas_call | solution.py:238
  25.5 0.8 %spectra_relay.1.refs_5_ = f32[2,272,256]{2,1,0:T(8,128)S(1)} custom-call(bf16[2,256,256]{2,1,0:T(8,128)(2,1)S(1)} %collective-permute-done.2.refs_0_, bf16[784,512]{1,0:T(8,128)(2,1)S(1)} %copy-done.1), custom_call_target="tpu_custom_call" | custom-call | flops 800000000 | bytes 1048576 | tf_op jit(solution)/shard_map/spectra_relay/pallas_call | solution.py:238
  26.4 0.0 copy-start.2
  26.4 0.0 collective-permute-done.7.refs_0_
  26.4 0.3 %collective-permute-done.8.refs_1_ = bf16[2,256,256]{2,1,0:T(8,128)(2,1)S(1)} collective-permute-done((bf16[2,256,256]{2,1,0:T(8,128)(2,1)S(1)}, bf16[2,256,256]{2,1,0:T(8,128)(2,1)S(1)}, u32[]{:S(2)}, u32[]{:S(2)}) %collective-permute-start.8) | collective-permute-done | bytes 262176 | tf_op jit(solution)/shard_map/ppermute | solution.py:286
  26.7 0.1 collective-permute-done.9.refs_6_
  26.8 0.2 copy-done.2
  27.0 1.4 %cross_other.1 = (bf16[4,272,256]{2,1,0:T(8,128)(2,1)S(1)}, f32[2,272,256]{2,1,0:T(8,128)S(1)}) custom-call(s32[2,8]{1,0:T(2,128)S(1)} %bitcast.7, f32[4,272,256]{2,1,0:T(8,128)S(1)} %spectra_own.1.refs_0_, f32[4,272,256]{2,1,0:T(8,128)S(1)} %spectra_swap.1.refs_1_, f32[4,272,256]{2,1,0:T(8,128)S(1)} %spectra_cross.1.refs_2_, ...), custom_call_target="tpu_custom_call" | custom-call | flops 536870912 | bytes 1048576 | tf_op jit(solution)/shard_map/cross_other/pallas_call | solution.py:238
  28.4 0.1 collective-permute-start.10
  28.5 0.0 copy-start.3
  28.5 0.0 copy-start.4
  28.5 1.0 %cross_mine.1.mine = bf16[4,272,256]{2,1,0:T(8,128)(2,1)S(1)} custom-call(s32[2,8]{1,0:T(2,128)S(1)} %bitcast.8, f32[4,272,256]{2,1,0:T(8,128)S(1)} %spectra_own.1.refs_0_, f32[4,272,256]{2,1,0:T(8,128)S(1)} %spectra_swap.1.refs_1_, f32[4,272,256]{2,1,0:T(8,128)S(1)} %spectra_cross.1.refs_2_, f32[4,272,256]{2,1,0:T(8,128)S(1)} %spectra_climb.1.refs_3_, ...), custom_call_target="tpu_custom_call" | custom-call | flops 33554432 | bytes 1048576 | tf_op jit(solution)/shard_map/cross_mine/pallas_call | solution.py:238
  29.5 0.9 %collective-permute-done.10.other = bf16[4,272,256]{2,1,0:T(8,128)(2,1)S(1)} collective-permute-done((bf16[4,272,256]{2,1,0:T(8,128)(2,1)S(1)}, bf16[4,272,256]{2,1,0:T(8,128)(2,1)S(1)}, u32[]{:S(2)}, u32[]{:S(2)}) %collective-permute-start.10) | collective-permute-done | bytes 557088 | tf_op jit(solution)/shard_map/ppermute | solution.py:305
  30.4 0.0 copy-done.3
  30.4 0.0 copy-done.4
  30.4 2.0 %surface.1 = (bf16[4,256,256]{2,1,0:T(8,128)(2,1)}, f32[4,8]{1,0:T(4,128)}) custom-call(s32[4,2,8]{2,1,0:T(2,128)S(1)} %bitcast.9, bf16[4,272,256]{2,1,0:T(8,128)(2,1)S(1)} %cross_mine.1.mine, bf16[4,272,256]{2,1,0:T(8,128)(2,1)S(1)} %collective-permute-done.10.other, bf16[768,512]{1,0:T(8,128)(2,1)S(1)} %copy-done.4), custom_call_target="tpu_custom_call" | custom-call | flops 1073741824 | bytes 1048576 | tf_op jit(solution)/shard_map/surface/pallas_call | solution.py:238
  (3 shorter events, 0.0 us)
Async XLA Ops:
  1.7 7.4 %collective-permute-start = (bf16[2,256,256]{2,1,0:T(8,128)(2,1)S(1)}, bf16[2,256,256]{2,1,0:T(8,128)(2,1)S(1)}, u32[]{:S(2)}, u32[]{:S(2)}) collective-permute-start(bf16[2,256,256]{2,1,0:T(8,128)(2,1)S(1)} %get-tuple-element.9.refs_0_), channel_id=1, source_target_pairs={{0,4},{1,3},{2,6},{3,1},{4,0},{5,7},{6,2},{7,5},{8,12},{9,11},{10,... | collective-permute-start | bytes 786440 | tf_op jit(solution)/shard_map/ppermute | solution.py:280
  4.7 8.5 %collective-permute-start.3 = (bf16[2,256,256]{2,1,0:T(8,128)(2,1)S(1)}, bf16[2,256,256]{2,1,0:T(8,128)(2,1)S(1)}, u32[]{:S(2)}, u32[]{:S(2)}) collective-permute-start(bf16[2,256,256]{2,1,0:T(8,128)(2,1)S(1)} %get-tuple-element.10.refs_1_), channel_id=1, source_target_pairs={{0,4},{1,3},{2,6},{3,1},{4,0},{5,7},{6,2},{7,5},{8,12},{9,11},{10,... | collective-permute-start | bytes 786440 | tf_op jit(solution)/shard_map/ppermute | solution.py:280
  4.8 1.1 %copy-start = (bf16[784,512]{1,0:T(8,128)(2,1)S(1)}, bf16[784,512]{1,0:T(8,128)(2,1)}, u32[]{:S(2)}) copy-start(bf16[784,512]{1,0:T(8,128)(2,1)} %constant.4.clone.refs_2_.refs_1_.refs_7_) | copy-start | bytes 2408452
  9.1 6.0 %collective-permute-start.1 = (bf16[2,256,256]{2,1,0:T(8,128)(2,1)S(1)}, bf16[2,256,256]{2,1,0:T(8,128)(2,1)S(1)}, u32[]{:S(2)}, u32[]{:S(2)}) collective-permute-start(bf16[2,256,256]{2,1,0:T(8,128)(2,1)S(1)} %collective-permute-done.first.refs_0_), channel_id=1, source_target_pairs={{0,8},{1,0},{2,10},{3,2},{4,5},{5,13},{6,7},{7,15},{8,16},{9,1},{1... | collective-permute-start | bytes 786440 | tf_op jit(solution)/shard_map/ppermute | solution.py:283
  11.2 6.4 %collective-permute-start.4 = (bf16[2,256,256]{2,1,0:T(8,128)(2,1)S(1)}, bf16[2,256,256]{2,1,0:T(8,128)(2,1)S(1)}, u32[]{:S(2)}, u32[]{:S(2)}) collective-permute-start(bf16[2,256,256]{2,1,0:T(8,128)(2,1)S(1)} %get-tuple-element.9.refs_0_), channel_id=1, source_target_pairs={{0,2},{1,5},{2,0},{3,7},{4,6},{5,1},{6,4},{7,3},{8,10},{9,13},{10,... | collective-permute-start | bytes 786440 | tf_op jit(solution)/shard_map/ppermute | solution.py:282
  12.7 7.7 %collective-permute-start.5 = (bf16[2,256,256]{2,1,0:T(8,128)(2,1)S(1)}, bf16[2,256,256]{2,1,0:T(8,128)(2,1)S(1)}, u32[]{:S(2)}, u32[]{:S(2)}) collective-permute-start(bf16[2,256,256]{2,1,0:T(8,128)(2,1)S(1)} %get-tuple-element.10.refs_1_), channel_id=1, source_target_pairs={{0,2},{1,5},{2,0},{3,7},{4,6},{5,1},{6,4},{7,3},{8,10},{9,13},{10,... | collective-permute-start | bytes 786440 | tf_op jit(solution)/shard_map/ppermute | solution.py:282
  13.2 7.2 %collective-permute-start.6 = (bf16[2,256,256]{2,1,0:T(8,128)(2,1)S(1)}, bf16[2,256,256]{2,1,0:T(8,128)(2,1)S(1)}, u32[]{:S(2)}, u32[]{:S(2)}) collective-permute-start(bf16[2,256,256]{2,1,0:T(8,128)(2,1)S(1)} %collective-permute-done.3.refs_1_.first), channel_id=1, source_target_pairs={{0,8},{1,0},{2,10},{3,2},{4,5},{5,13},{6,7},{7,15},{8,16},{9,1},{1... | collective-permute-start | bytes 786440 | tf_op jit(solution)/shard_map/ppermute | solution.py:283
  15.1 6.9 %copy-start.1 = (bf16[784,512]{1,0:T(8,128)(2,1)S(1)}, bf16[784,512]{1,0:T(8,128)(2,1)}, u32[]{:S(2)}) copy-start(bf16[784,512]{1,0:T(8,128)(2,1)} %constant.4.clone.refs_2_.refs_1_.refs_7_) | copy-start | bytes 2408452
  15.1 8.1 %collective-permute-start.2 = (bf16[2,256,256]{2,1,0:T(8,128)(2,1)S(1)}, bf16[2,256,256]{2,1,0:T(8,128)(2,1)S(1)}, u32[]{:S(2)}, u32[]{:S(2)}) collective-permute-start(bf16[2,256,256]{2,1,0:T(8,128)(2,1)S(1)} %choose.2), channel_id=1, source_target_pairs={{0,2},{1,5},{2,0},{3,7},{4,6},{5,1},{6,4},{7,3},{8,10},{9,13},{10,... | collective-permute-start | bytes 786440 | tf_op jit(solution)/shard_map/ppermute | solution.py:285
  17.5 8.8 %collective-permute-start.7 = (bf16[2,256,256]{2,1,0:T(8,128)(2,1)S(1)}, bf16[2,256,256]{2,1,0:T(8,128)(2,1)S(1)}, u32[]{:S(2)}, u32[]{:S(2)}) collective-permute-start(bf16[2,256,256]{2,1,0:T(8,128)(2,1)S(1)} %collective-permute-done.4.refs_0_), channel_id=1, source_target_pairs={{0,1},{1,9},{2,3},{3,11},{4,12},{5,4},{6,14},{7,6},{8,0},{9,17},{1... | collective-permute-start | bytes 786440 | tf_op jit(solution)/shard_map/ppermute | solution.py:286
  20.3 6.4 %collective-permute-start.8 = (bf16[2,256,256]{2,1,0:T(8,128)(2,1)S(1)}, bf16[2,256,256]{2,1,0:T(8,128)(2,1)S(1)}, u32[]{:S(2)}, u32[]{:S(2)}) collective-permute-start(bf16[2,256,256]{2,1,0:T(8,128)(2,1)S(1)} %collective-permute-done.5.refs_1_), channel_id=1, source_target_pairs={{0,1},{1,9},{2,3},{3,11},{4,12},{5,4},{6,14},{7,6},{8,0},{9,17},{1... | collective-permute-start | bytes 786440 | tf_op jit(solution)/shard_map/ppermute | solution.py:286
  20.4 6.4 %collective-permute-start.9 = (bf16[2,256,256]{2,1,0:T(8,128)(2,1)S(1)}, bf16[2,256,256]{2,1,0:T(8,128)(2,1)S(1)}, u32[]{:S(2)}, u32[]{:S(2)}) collective-permute-start(bf16[2,256,256]{2,1,0:T(8,128)(2,1)S(1)} %choose.3), channel_id=1, source_target_pairs={{0,2},{1,5},{2,0},{3,7},{4,6},{5,1},{6,4},{7,3},{8,10},{9,13},{10,... | collective-permute-start | bytes 786440 | tf_op jit(solution)/shard_map/ppermute | solution.py:285
  26.4 0.7 %copy-start.2 = (s32[8,2]{0,1:T(2,128)S(1)}, s32[8,2]{0,1:T(2,128)}, u32[]{:S(2)}) copy-start(s32[8,2]{0,1:T(2,128)} %param.6) | copy-start | bytes 196
  28.4 2.0 %collective-permute-start.10 = (bf16[4,272,256]{2,1,0:T(8,128)(2,1)S(1)}, bf16[4,272,256]{2,1,0:T(8,128)(2,1)S(1)}, u32[]{:S(2)}, u32[]{:S(2)}) collective-permute-start(bf16[4,272,256]{2,1,0:T(8,128)(2,1)S(1)} %get-tuple-element.13), channel_id=1, source_target_pairs={{0,1},{1,0},{2,3},{3,2},{4,5},{5,4},{6,7},{7,6},{8,9},{9,8},{10,11... | collective-permute-start | bytes 1671176 | tf_op jit(solution)/shard_map/ppermute | solution.py:305
  28.5 1.9 %copy-start.3 = (s32[4,8,2]{1,2,0:T(2,128)S(1)}, s32[4,8,2]{1,2,0:T(2,128)}, u32[]{:S(2)}) copy-start(s32[4,8,2]{1,2,0:T(2,128)} %param.7) | copy-start | bytes 772
  28.5 1.9 %copy-start.4 = (bf16[768,512]{1,0:T(8,128)(2,1)S(1)}, bf16[768,512]{1,0:T(8,128)(2,1)}, u32[]{:S(2)}) copy-start(bf16[768,512]{1,0:T(8,128)(2,1)} %constant.5.clone.table) | copy-start | bytes 2359300

commit v2 on v1

--- a/solution.py
+++ b/solution.py
@@ -110,17 +110,19 @@
     return jnp.concatenate(parts, axis=0).astype(jnp.bfloat16)
 
 
-def write_crosses(first_pair, cuts, ends, blocks, out, taken):
+def write_crosses(first_pair, cuts, ends, blocks, out):
     here = lax.axis_index("tile")
     held = distances(here, lax.axis_index("chan"))
     own = blocks[0]
     tile_dev = own.shape[0]
-    half = taken.shape[-1] // 2
-    count = out.shape[0]
-    for k in range(count):
-        tile = ends[1, first_pair + k]
+    half = out.shape[-1] // 2
+
+    for k in range(out.shape[0]):
+        pair = first_pair + k
+        tile = ends[1, pair]
         away = tile // tile_dev - here
         slot = tile % tile_dev
+        mine = ends[0, pair] - here * tile_dev
         for (index, base), source in zip(cuts, blocks):
             size = source.shape[0]
             pick = away == held[index]
@@ -129,50 +131,50 @@
 
             @pl.when(pick)
             def _(source=source, base=base):
-                taken[k] = source[slot - base]
-
-    for k in range(count):
-        out[k] = cross_slab(own[ends[0, first_pair + k] - here * tile_dev], taken[k], half)
+                out[k] = cross_slab(own[mine], source[slot - base], half)
 
 
 def cross_other_kernel(cuts, ends, *refs):
-    blocks, (panels, table, out, slabs, taken, numbers, sem) = refs[: len(cuts) - 1], refs[len(cuts) - 1 :]
+    blocks, (panels, table, out, slabs, numbers, sem) = refs[: len(cuts) - 1], refs[len(cuts) - 1 :]
     copy = pltpu.make_async_copy(ends, numbers, sem)
     copy.start()
     for k, slab in enumerate(spectra_of(panels[...], table)):
         slabs[k] = slab
     copy.wait()
     first_pair = out.shape[0] * (1 - lax.axis_index("chan"))
-    write_crosses(first_pair, cuts, numbers, (*blocks, slabs), out, taken)
+    write_crosses(first_pair, cuts, numbers, (*blocks, slabs), out)
 
 
 def cross_mine_kernel(cuts, ends, *refs):
-    blocks, (out, taken) = refs[: len(cuts)], refs[len(cuts) :]
-    write_crosses(out.shape[0] * lax.axis_index("chan"), cuts, ends, blocks, out, taken)
-
-
-def surface_kernel(spots, mine, other, table, surface, scores, corr, peaks, sem):
-    copy = pltpu.make_async_copy(spots, peaks, sem)
-    copy.start()
+    blocks, out = refs[: len(cuts)], refs[len(cuts)]
+    write_crosses(out.shape[0] * lax.axis_index("chan"), cuts, ends, blocks, out)
+
+
+def quotient(slab, half):
+    real, imag, real_x, imag_x = split(slab, half)
+    magnitude = jnp.sqrt(real * real + imag * imag)
+    magnitude_x = jnp.sqrt(real_x * real_x + imag_x * imag_x)
+    columns = 2.0 * jnp.sum(magnitude, axis=0, keepdims=True) - magnitude[:1]
+    columns = columns + jnp.sum(magnitude_x, axis=0, keepdims=True)
+    level = jnp.sum(columns, axis=1, keepdims=True) / (4 * half * half) + 1e-06
+    scale = 1.0 / (magnitude + FLOOR * level)
+    scale_x = 1.0 / (magnitude_x + FLOOR * level)
+    q_real = jnp.concatenate([real * scale, real_x * scale_x], axis=0)
+    q_imag = jnp.concatenate([imag * scale, imag_x * scale_x], axis=0)
+    return jnp.concatenate([q_real, q_imag], axis=1)
+
+
+def surface_kernel(spots, mine, other, table, surface, scores, corr, rounded, found, peaks, sem, sems):
+    fetch = pltpu.make_async_copy(spots, peaks, sem)
+    fetch.start()
     count, _, size = surface.shape
     cand = scores.shape[1]
     half = size // 2
-    parts = []
-    for k in range(count):
-        slab = mine[k].astype(jnp.float32) + other[k].astype(jnp.float32)
-        real, imag, real_x, imag_x = split(slab, half)
-        magnitude = jnp.sqrt(real * real + imag * imag)
-        magnitude_x = jnp.sqrt(real_x * real_x + imag_x * imag_x)
-        total = 2.0 * jnp.sum(magnitude) - jnp.sum(magnitude[:1]) + jnp.sum(magnitude_x)
-        level = total / (size * size) + 1e-06
-        scale = 1.0 / (magnitude + FLOOR * level)
-        scale_x = 1.0 / (magnitude_x + FLOOR * level)
-        q_real = jnp.concatenate([real * scale, real_x * scale_x], axis=0)
-        q_imag = jnp.concatenate([imag * scale, imag_x * scale_x], axis=0)
-        parts.append(jnp.concatenate([q_real, q_imag], axis=1))
+    parts = [quotient(mine[k].astype(jnp.float32) + other[k].astype(jnp.float32), half) for k in range(count)]
     spread = half + EXTRA
     y_all = product(jnp.concatenate(parts, axis=0).astype(jnp.bfloat16), table[: 2 * size])
     last = table[2 * size :, :size]
+    copies = []
     for k in range(count):
         y = y_all[k * spread : (k + 1) * spread]
         y_real = y[:half, :size]
@@ -182,8 +184,10 @@
         both = jnp.concatenate([y_real, y_imag], axis=0).astype(jnp.bfloat16)
         result = product(last, both)
         corr[k] = result
-        surface[k] = result.astype(jnp.bfloat16)
-    copy.wait()
+        rounded[k] = result.astype(jnp.bfloat16)
+        copies.append(pltpu.make_async_copy(rounded.at[k], surface.at[k], sems.at[k]))
+        copies[-1].start()
+    fetch.wait()
     lane = lax.broadcasted_iota(jnp.int32, (1, size), 1)
     diagonal = lax.broadcasted_iota(jnp.int32, (cand, cand), 0) == lax.broadcasted_iota(jnp.int32, (cand, cand), 1)
     for k in range(count):
@@ -191,8 +195,12 @@
         for j in range(cand):
             row = corr[k, pl.ds(peaks[k, 0, j], 1), :]
             picked.append(jnp.where(lane == peaks[k, 1, j], row, 0.0))
-        found = jnp.sum(jnp.concatenate(picked, axis=0), axis=1, keepdims=True)
-        scores[k : k + 1, :] = jnp.sum(jnp.where(diagonal, found, 0.0), axis=0, keepdims=True)
+        sums = jnp.sum(jnp.concatenate(picked, axis=0), axis=1, keepdims=True)
+        found[k : k + 1, :] = jnp.sum(jnp.where(diagonal, sums, 0.0), axis=0, keepdims=True)
+    copies.append(pltpu.make_async_copy(found, scores, sems.at[count]))
+    copies[-1].start()
+    for copy in copies:
+        copy.wait()
 
 
 def choose_kernel(first, second, out):
@@ -234,12 +242,12 @@
     return lax.optimization_barrier((value, *earlier))[0]
 
 
-def call(kernel, name, operands, out, scratch=(), first=VMEM, flops=1 << 30):
+def call(kernel, name, operands, out, scratch=(), first=VMEM, flops=1 << 30, results=VMEM):
     return pl.pallas_call(
         kernel,
         out_shape=out,
         in_specs=[first] + [VMEM] * (len(operands) - 1),
-        out_specs=jax.tree.map(lambda _: VMEM, out),
+        out_specs=jax.tree.map(lambda _: results, out),
         scratch_shapes=scratch,
         compiler_params=pltpu.CompilerParams(vmem_limit_bytes=8 << 20),
         cost_estimate=pl.CostEstimate(flops=flops, bytes_accessed=1 << 20, transcendentals=0),
@@ -292,13 +300,12 @@
     blocks = [own, from_swap, from_cross, from_climb, from_late, from_relay]
     cuts = [(index, 0) for index in range(len(blocks))] + [(len(blocks) - 1, half)]
     crosses = jax.ShapeDtypeStruct((share, slab, size), jnp.bfloat16)
-    taken = pltpu.VMEM((share, slab, size), jnp.float32)
     given, last = call(
         functools.partial(cross_other_kernel, cuts),
         "cross_other",
         (ends, *blocks, got_relay[1], forward),
         (crosses, jax.ShapeDtypeStruct((tile_dev - half, slab, size), jnp.float32)),
-        [taken, pltpu.SMEM(ends.shape, ends.dtype), pltpu.SemaphoreType.DMA(())],
+        [pltpu.SMEM(ends.shape, ends.dtype), pltpu.SemaphoreType.DMA(())],
         ANY,
         flops=1 << 29,
     )
@@ -308,8 +315,7 @@
         "cross_mine",
         (ends, *blocks, last),
         crosses,
-        [taken],
-        SMEM,
+        first=SMEM,
         flops=1 << 25,
     )
     return call(
@@ -317,8 +323,16 @@
         "surface",
         (spots, kept, other, backward),
         (jax.ShapeDtypeStruct((share, size, size), jnp.bfloat16), jax.ShapeDtypeStruct((share, cand), jnp.float32)),
-        [pltpu.VMEM((share, size, size), jnp.float32), pltpu.SMEM(spots.shape, spots.dtype), pltpu.SemaphoreType.DMA(())],
+        [
+            pltpu.VMEM((share, size, size), jnp.float32),
+            pltpu.VMEM((share, size, size), jnp.bfloat16),
+            pltpu.VMEM((share, cand), jnp.float32),
+            pltpu.SMEM(spots.shape, spots.dtype),
+            pltpu.SemaphoreType.DMA(()),
+            pltpu.SemaphoreType.DMA((share + 1,)),
+        ],
         ANY,
+        results=ANY,
     )
 
 

time: 32.6 us -> 32.3 us (level)
  Pallas kernels: 9.93 us -> 9.49 us
    pallas_call x11, Pallas kernels: 9.93 us -> 9.49 us  [call(): pl.pallas_call(kernel, out_shape=out, in_specs=[first] + [VMEM] * (len(op...]
where the time goes in v2:
time: 32.3 us; the launch traced here: 32.1 us
  starting transfers between devices  12 us (37%)
  Pallas kernels  9.49 us (29%)
  waiting for transfers between devices  7.44 us (23%)
  local copies, waits for them, and re-layouts  2.45 us (8%)
  between operations  0.76 us (2%)
    pallas_call x11, Pallas kernels, call(): pl.pallas_call(kernel, out_shape=out, in_specs=[first] + [VMEM] * (len(op...  9.49 us
    ppermute x2, waiting for transfers between devices, shards(): move(after(part, got_swap[0], own), perm=cross_swap)  3.7 us
    ppermute x2, starting transfers between devices, shards(): got_climb = [move(part, perm=climb) for part in got_swap]  3.65 us
    ppermute x2, starting transfers between devices, shards(): got_swap = [move(part, perm=swap) for part in parts]  3.11 us
    ppermute x2, starting transfers between devices, shards(): got_relay = [move(part, perm=relay) for part in picked]  3.11 us
    ppermute x2, starting transfers between devices, shards(): move(after(part, got_swap[0], own), perm=cross_swap)  2.03 us
    ppermute x2, waiting for transfers between devices, shards(): got_swap = [move(part, perm=swap) for part in parts]  1.97 us
    unnamed x10, local copies, waits for them, and re-layouts  1.39 us
  transfers between devices with their start and end apart: 11, of which 7 were waited for; matrix products, arithmetic and copies ran while one was open for 0% of the time, Pallas kernels for 20%

profile of v2, /device:TPU:0, one launch (start us, length us, event | category | flops | bytes accessed | tf_op | source)
XLA Modules:
  0.0 32.1 jit_solution(2784426345375694952)
XLA Ops:
  0.6 1.1 %slice_bitcast_fusion = (bf16[2,256,256]{2,1,0:T(8,128)(2,1)S(1)}, bf16[2,256,256]{2,1,0:T(8,128)(2,1)S(1)}) fusion(bf16[4,1,256,256]{3,2,0,1:T(8,128)(2,1)} %bitcast.10), kind=kLoop, calls=%fused_computation | loop fusion | bytes 1048576 | tf_op jit(solution)/shard_map/slice | solution.py:287
  1.7 3.0 %collective-permute-start = (bf16[2,256,256]{2,1,0:T(8,128)(2,1)S(1)}, bf16[2,256,256]{2,1,0:T(8,128)(2,1)S(1)}, u32[]{:S(2)}, u32[]{:S(2)}) collective-permute-start(bf16[2,256,256]{2,1,0:T(8,128)(2,1)S(1)} %get-tuple-element.9.refs_0_), channel_id=1, source_target_pairs={{0,4},{1,3},{2,6},{3,1},{4,0},{5,7},{6,2},{7,5},{8,12},{9,11},{10,... | collective-permute-start | bytes 786440 | tf_op jit(solution)/shard_map/ppermute | solution.py:288
  4.7 0.1 collective-permute-start.3
  4.8 0.0 copy-start
  4.8 1.1 %copy-done = bf16[784,512]{1,0:T(8,128)(2,1)S(1)} copy-done((bf16[784,512]{1,0:T(8,128)(2,1)S(1)}, bf16[784,512]{1,0:T(8,128)(2,1)}, u32[]{:S(2)}) %copy-start) | copy-done | bytes 802840
  5.9 1.2 %spectra_own.1.refs_0_ = f32[4,272,256]{2,1,0:T(8,128)S(1)} custom-call(bf16[2,256,256]{2,1,0:T(8,128)(2,1)S(1)} %get-tuple-element.9.refs_0_, bf16[2,256,256]{2,1,0:T(8,128)(2,1)S(1)} %get-tuple-element.10.refs_1_, bf16[784,512]{1,0:T(8,128)(2,1)S(1)} %copy-done), custom_call_target="tpu_custom_call" | custom-call | flops 805306368 | bytes 1048576 | tf_op jit(solution)/shard_map/spectra_own/pallas_call | solution.py:246
  7.1 2.0 %collective-permute-done.first.refs_0_ = bf16[2,256,256]{2,1,0:T(8,128)(2,1)S(1)} collective-permute-done((bf16[2,256,256]{2,1,0:T(8,128)(2,1)S(1)}, bf16[2,256,256]{2,1,0:T(8,128)(2,1)S(1)}, u32[]{:S(2)}, u32[]{:S(2)}) %collective-permute-start) | collective-permute-done | bytes 262176 | tf_op jit(solution)/shard_map/ppermute | solution.py:288
  9.1 2.1 %collective-permute-start.1 = (bf16[2,256,256]{2,1,0:T(8,128)(2,1)S(1)}, bf16[2,256,256]{2,1,0:T(8,128)(2,1)S(1)}, u32[]{:S(2)}, u32[]{:S(2)}) collective-permute-start(bf16[2,256,256]{2,1,0:T(8,128)(2,1)S(1)} %collective-permute-done.first.refs_0_), channel_id=1, source_target_pairs={{0,8},{1,0},{2,10},{3,2},{4,5},{5,13},{6,7},{7,15},{8,16},{9,1},{1... | collective-permute-start | bytes 786440 | tf_op jit(solution)/shard_map/ppermute | solution.py:291
  11.2 1.5 %collective-permute-start.4 = (bf16[2,256,256]{2,1,0:T(8,128)(2,1)S(1)}, bf16[2,256,256]{2,1,0:T(8,128)(2,1)S(1)}, u32[]{:S(2)}, u32[]{:S(2)}) collective-permute-start(bf16[2,256,256]{2,1,0:T(8,128)(2,1)S(1)} %get-tuple-element.9.refs_0_), channel_id=1, source_target_pairs={{0,2},{1,5},{2,0},{3,7},{4,6},{5,1},{6,4},{7,3},{8,10},{9,13},{10,... | collective-permute-start | bytes 786440 | tf_op jit(solution)/shard_map/ppermute | solution.py:290
  12.7 0.5 %collective-permute-start.5 = (bf16[2,256,256]{2,1,0:T(8,128)(2,1)S(1)}, bf16[2,256,256]{2,1,0:T(8,128)(2,1)S(1)}, u32[]{:S(2)}, u32[]{:S(2)}) collective-permute-start(bf16[2,256,256]{2,1,0:T(8,128)(2,1)S(1)} %get-tuple-element.10.refs_1_), channel_id=1, source_target_pairs={{0,2},{1,5},{2,0},{3,7},{4,6},{5,1},{6,4},{7,3},{8,10},{9,13},{10,... | collective-permute-start | bytes 786440 | tf_op jit(solution)/shard_map/ppermute | solution.py:290
  13.2 0.0 collective-permute-done.3.refs_1_.first
  13.2 1.6 %collective-permute-start.6 = (bf16[2,256,256]{2,1,0:T(8,128)(2,1)S(1)}, bf16[2,256,256]{2,1,0:T(8,128)(2,1)S(1)}, u32[]{:S(2)}, u32[]{:S(2)}) collective-permute-start(bf16[2,256,256]{2,1,0:T(8,128)(2,1)S(1)} %collective-permute-done.3.refs_1_.first), channel_id=1, source_target_pairs={{0,8},{1,0},{2,10},{3,2},{4,5},{5,13},{6,7},{7,15},{8,16},{9,1},{1... | collective-permute-start | bytes 786440 | tf_op jit(solution)/shard_map/ppermute | solution.py:291
  14.8 0.3 collective-permute-done.1.second.refs_0_
  15.1 0.0 copy-start.1
  15.1 1.6 %collective-permute-start.2 = (bf16[2,256,256]{2,1,0:T(8,128)(2,1)S(1)}, bf16[2,256,256]{2,1,0:T(8,128)(2,1)S(1)}, u32[]{:S(2)}, u32[]{:S(2)}) collective-permute-start(bf16[2,256,256]{2,1,0:T(8,128)(2,1)S(1)} %choose.2), channel_id=1, source_target_pairs={{0,2},{1,5},{2,0},{3,7},{4,6},{5,1},{6,4},{7,3},{8,10},{9,13},{10,... | collective-permute-start | bytes 786440 | tf_op jit(solution)/shard_map/ppermute | solution.py:293
  16.6 0.9 %collective-permute-done.4.refs_0_ = bf16[2,256,256]{2,1,0:T(8,128)(2,1)S(1)} collective-permute-done((bf16[2,256,256]{2,1,0:T(8,128)(2,1)S(1)}, bf16[2,256,256]{2,1,0:T(8,128)(2,1)S(1)}, u32[]{:S(2)}, u32[]{:S(2)}) %collective-permute-start.4) | collective-permute-done | bytes 262176 | tf_op jit(solution)/shard_map/ppermute | solution.py:290
  17.5 0.0 collective-permute-start.7
  17.5 2.8 %collective-permute-done.5.refs_1_ = bf16[2,256,256]{2,1,0:T(8,128)(2,1)S(1)} collective-permute-done((bf16[2,256,256]{2,1,0:T(8,128)(2,1)S(1)}, bf16[2,256,256]{2,1,0:T(8,128)(2,1)S(1)}, u32[]{:S(2)}, u32[]{:S(2)}) %collective-permute-start.5) | collective-permute-done | bytes 262176 | tf_op jit(solution)/shard_map/ppermute | solution.py:290
  20.3 0.0 collective-permute-start.8
  20.3 0.0 collective-permute-done.6.refs_1_.second
  20.4 1.6 %collective-permute-start.9 = (bf16[2,256,256]{2,1,0:T(8,128)(2,1)S(1)}, bf16[2,256,256]{2,1,0:T(8,128)(2,1)S(1)}, u32[]{:S(2)}, u32[]{:S(2)}) collective-permute-start(bf16[2,256,256]{2,1,0:T(8,128)(2,1)S(1)} %choose.3), channel_id=1, source_target_pairs={{0,2},{1,5},{2,0},{3,7},{4,6},{5,1},{6,4},{7,3},{8,10},{9,13},{10,... | collective-permute-start | bytes 786440 | tf_op jit(solution)/shard_map/ppermute | solution.py:293
  21.9 0.0 copy-done.1
  21.9 1.2 %spectra_cross.1.refs_2_ = f32[4,272,256]{2,1,0:T(8,128)S(1)} custom-call(bf16[2,256,256]{2,1,0:T(8,128)(2,1)S(1)} %collective-permute-done.4.refs_0_, bf16[2,256,256]{2,1,0:T(8,128)(2,1)S(1)} %collective-permute-done.5.refs_1_, bf16[784,512]{1,0:T(8,128)(2,1)S(1)} %copy-done.1), custom_call_target="tpu_custom_call" | custom-call | flops 1000000 | bytes 1048576 | tf_op jit(solution)/shard_map/spectra_cross/pallas_call | solution.py:246
  23.1 0.0 collective-permute-done.2.refs_0_
  23.1 1.2 %spectra_swap.1.refs_1_ = f32[4,272,256]{2,1,0:T(8,128)S(1)} custom-call(bf16[2,256,256]{2,1,0:T(8,128)(2,1)S(1)} %collective-permute-done.first.refs_0_, bf16[2,256,256]{2,1,0:T(8,128)(2,1)S(1)} %collective-permute-done.3.refs_1_.first, bf16[784,512]{1,0:T(8,128)(2,1)S(1)} %copy-done.1), custom_call_target="tpu_custom_call" | custom-call | flops 805306368 | bytes 1048576 | tf_op jit(solution)/shard_map/spectra_swap/pallas_call | solution.py:246
  24.3 1.2 %spectra_climb.1.refs_3_ = f32[4,272,256]{2,1,0:T(8,128)S(1)} custom-call(bf16[2,256,256]{2,1,0:T(8,128)(2,1)S(1)} %collective-permute-done.1.second.refs_0_, bf16[2,256,256]{2,1,0:T(8,128)(2,1)S(1)} %collective-permute-done.6.refs_1_.second, bf16[784,512]{1,0:T(8,128)(2,1)S(1)} %copy-done.1), custom_call_target="tpu_custom_call" | custom-call | flops 1000000 | bytes 1048576 | tf_op jit(solution)/shard_map/spectra_climb/pallas_call | solution.py:246
  25.5 0.8 %spectra_relay.1.refs_5_ = f32[2,272,256]{2,1,0:T(8,128)S(1)} custom-call(bf16[2,256,256]{2,1,0:T(8,128)(2,1)S(1)} %collective-permute-done.2.refs_0_, bf16[784,512]{1,0:T(8,128)(2,1)S(1)} %copy-done.1), custom_call_target="tpu_custom_call" | custom-call | flops 800000000 | bytes 1048576 | tf_op jit(solution)/shard_map/spectra_relay/pallas_call | solution.py:246
  26.4 0.0 copy-start.2
  26.4 0.0 collective-permute-done.7.refs_0_
  26.4 0.3 %collective-permute-done.8.refs_1_ = bf16[2,256,256]{2,1,0:T(8,128)(2,1)S(1)} collective-permute-done((bf16[2,256,256]{2,1,0:T(8,128)(2,1)S(1)}, bf16[2,256,256]{2,1,0:T(8,128)(2,1)S(1)}, u32[]{:S(2)}, u32[]{:S(2)}) %collective-permute-start.8) | collective-permute-done | bytes 262176 | tf_op jit(solution)/shard_map/ppermute | solution.py:294
  26.7 0.1 collective-permute-done.9.refs_6_
  26.8 0.2 copy-done.2
  27.0 1.2 %cross_other.1 = (bf16[4,272,256]{2,1,0:T(8,128)(2,1)S(1)}, f32[2,272,256]{2,1,0:T(8,128)S(1)}) custom-call(s32[2,8]{1,0:T(2,128)S(1)} %bitcast.7, f32[4,272,256]{2,1,0:T(8,128)S(1)} %spectra_own.1.refs_0_, f32[4,272,256]{2,1,0:T(8,128)S(1)} %spectra_swap.1.refs_1_, f32[4,272,256]{2,1,0:T(8,128)S(1)} %spectra_cross.1.refs_2_, ...), custom_call_target="tpu_custom_call" | custom-call | flops 536870912 | bytes 1048576 | tf_op jit(solution)/shard_map/cross_other/pallas_call | solution.py:246
  28.3 0.1 collective-permute-start.10
  28.3 0.0 copy-start.3
  28.4 0.0 copy-start.4
  28.4 0.9 %cross_mine.1.mine = bf16[4,272,256]{2,1,0:T(8,128)(2,1)S(1)} custom-call(s32[2,8]{1,0:T(2,128)S(1)} %bitcast.8, f32[4,272,256]{2,1,0:T(8,128)S(1)} %spectra_own.1.refs_0_, f32[4,272,256]{2,1,0:T(8,128)S(1)} %spectra_swap.1.refs_1_, f32[4,272,256]{2,1,0:T(8,128)S(1)} %spectra_cross.1.refs_2_, f32[4,272,256]{2,1,0:T(8,128)S(1)} %spectra_climb.1.refs_3_, ...), custom_call_target="tpu_custom_call" | custom-call | flops 33554432 | bytes 1048576 | tf_op jit(solution)/shard_map/cross_mine/pallas_call | solution.py:246
  29.3 1.0 %collective-permute-done.10.other = bf16[4,272,256]{2,1,0:T(8,128)(2,1)S(1)} collective-permute-done((bf16[4,272,256]{2,1,0:T(8,128)(2,1)S(1)}, bf16[4,272,256]{2,1,0:T(8,128)(2,1)S(1)}, u32[]{:S(2)}, u32[]{:S(2)}) %collective-permute-start.10) | collective-permute-done | bytes 557088 | tf_op jit(solution)/shard_map/ppermute | solution.py:312
  30.3 0.0 copy-done.3
  30.3 0.0 copy-done.4
  30.3 1.8 %surface.1 = (bf16[4,256,256]{2,1,0:T(8,128)(2,1)}, f32[4,8]{1,0:T(4,128)}) custom-call(s32[4,2,8]{2,1,0:T(2,128)S(1)} %bitcast.9, bf16[4,272,256]{2,1,0:T(8,128)(2,1)S(1)} %cross_mine.1.mine, bf16[4,272,256]{2,1,0:T(8,128)(2,1)S(1)} %collective-permute-done.10.other, bf16[768,512]{1,0:T(8,128)(2,1)S(1)} %copy-done.4), custom_call_target="tpu_custom_call" | custom-call | flops 1073741824 | bytes 1048576 | tf_op jit(solution)/shard_map/surface/pallas_call | solution.py:246
  (3 shorter events, 0.0 us)
Async XLA Ops:
  1.7 7.4 %collective-permute-start = (bf16[2,256,256]{2,1,0:T(8,128)(2,1)S(1)}, bf16[2,256,256]{2,1,0:T(8,128)(2,1)S(1)}, u32[]{:S(2)}, u32[]{:S(2)}) collective-permute-start(bf16[2,256,256]{2,1,0:T(8,128)(2,1)S(1)} %get-tuple-element.9.refs_0_), channel_id=1, source_target_pairs={{0,4},{1,3},{2,6},{3,1},{4,0},{5,7},{6,2},{7,5},{8,12},{9,11},{10,... | collective-permute-start | bytes 786440 | tf_op jit(solution)/shard_map/ppermute | solution.py:288
  4.7 8.5 %collective-permute-start.3 = (bf16[2,256,256]{2,1,0:T(8,128)(2,1)S(1)}, bf16[2,256,256]{2,1,0:T(8,128)(2,1)S(1)}, u32[]{:S(2)}, u32[]{:S(2)}) collective-permute-start(bf16[2,256,256]{2,1,0:T(8,128)(2,1)S(1)} %get-tuple-element.10.refs_1_), channel_id=1, source_target_pairs={{0,4},{1,3},{2,6},{3,1},{4,0},{5,7},{6,2},{7,5},{8,12},{9,11},{10,... | collective-permute-start | bytes 786440 | tf_op jit(solution)/shard_map/ppermute | solution.py:288
  4.8 1.1 %copy-start = (bf16[784,512]{1,0:T(8,128)(2,1)S(1)}, bf16[784,512]{1,0:T(8,128)(2,1)}, u32[]{:S(2)}) copy-start(bf16[784,512]{1,0:T(8,128)(2,1)} %constant.4.clone.refs_2_.refs_1_.refs_7_) | copy-start | bytes 2408452
  9.1 6.0 %collective-permute-start.1 = (bf16[2,256,256]{2,1,0:T(8,128)(2,1)S(1)}, bf16[2,256,256]{2,1,0:T(8,128)(2,1)S(1)}, u32[]{:S(2)}, u32[]{:S(2)}) collective-permute-start(bf16[2,256,256]{2,1,0:T(8,128)(2,1)S(1)} %collective-permute-done.first.refs_0_), channel_id=1, source_target_pairs={{0,8},{1,0},{2,10},{3,2},{4,5},{5,13},{6,7},{7,15},{8,16},{9,1},{1... | collective-permute-start | bytes 786440 | tf_op jit(solution)/shard_map/ppermute | solution.py:291
  11.2 6.4 %collective-permute-start.4 = (bf16[2,256,256]{2,1,0:T(8,128)(2,1)S(1)}, bf16[2,256,256]{2,1,0:T(8,128)(2,1)S(1)}, u32[]{:S(2)}, u32[]{:S(2)}) collective-permute-start(bf16[2,256,256]{2,1,0:T(8,128)(2,1)S(1)} %get-tuple-element.9.refs_0_), channel_id=1, source_target_pairs={{0,2},{1,5},{2,0},{3,7},{4,6},{5,1},{6,4},{7,3},{8,10},{9,13},{10,... | collective-permute-start | bytes 786440 | tf_op jit(solution)/shard_map/ppermute | solution.py:290
  12.7 7.7 %collective-permute-start.5 = (bf16[2,256,256]{2,1,0:T(8,128)(2,1)S(1)}, bf16[2,256,256]{2,1,0:T(8,128)(2,1)S(1)}, u32[]{:S(2)}, u32[]{:S(2)}) collective-permute-start(bf16[2,256,256]{2,1,0:T(8,128)(2,1)S(1)} %get-tuple-element.10.refs_1_), channel_id=1, source_target_pairs={{0,2},{1,5},{2,0},{3,7},{4,6},{5,1},{6,4},{7,3},{8,10},{9,13},{10,... | collective-permute-start | bytes 786440 | tf_op jit(solution)/shard_map/ppermute | solution.py:290
  13.2 7.2 %collective-permute-start.6 = (bf16[2,256,256]{2,1,0:T(8,128)(2,1)S(1)}, bf16[2,256,256]{2,1,0:T(8,128)(2,1)S(1)}, u32[]{:S(2)}, u32[]{:S(2)}) collective-permute-start(bf16[2,256,256]{2,1,0:T(8,128)(2,1)S(1)} %collective-permute-done.3.refs_1_.first), channel_id=1, source_target_pairs={{0,8},{1,0},{2,10},{3,2},{4,5},{5,13},{6,7},{7,15},{8,16},{9,1},{1... | collective-permute-start | bytes 786440 | tf_op jit(solution)/shard_map/ppermute | solution.py:291
  15.1 6.9 %copy-start.1 = (bf16[784,512]{1,0:T(8,128)(2,1)S(1)}, bf16[784,512]{1,0:T(8,128)(2,1)}, u32[]{:S(2)}) copy-start(bf16[784,512]{1,0:T(8,128)(2,1)} %constant.4.clone.refs_2_.refs_1_.refs_7_) | copy-start | bytes 2408452
  15.1 8.1 %collective-permute-start.2 = (bf16[2,256,256]{2,1,0:T(8,128)(2,1)S(1)}, bf16[2,256,256]{2,1,0:T(8,128)(2,1)S(1)}, u32[]{:S(2)}, u32[]{:S(2)}) collective-permute-start(bf16[2,256,256]{2,1,0:T(8,128)(2,1)S(1)} %choose.2), channel_id=1, source_target_pairs={{0,2},{1,5},{2,0},{3,7},{4,6},{5,1},{6,4},{7,3},{8,10},{9,13},{10,... | collective-permute-start | bytes 786440 | tf_op jit(solution)/shard_map/ppermute | solution.py:293
  17.5 8.8 %collective-permute-start.7 = (bf16[2,256,256]{2,1,0:T(8,128)(2,1)S(1)}, bf16[2,256,256]{2,1,0:T(8,128)(2,1)S(1)}, u32[]{:S(2)}, u32[]{:S(2)}) collective-permute-start(bf16[2,256,256]{2,1,0:T(8,128)(2,1)S(1)} %collective-permute-done.4.refs_0_), channel_id=1, source_target_pairs={{0,1},{1,9},{2,3},{3,11},{4,12},{5,4},{6,14},{7,6},{8,0},{9,17},{1... | collective-permute-start | bytes 786440 | tf_op jit(solution)/shard_map/ppermute | solution.py:294
  20.3 6.4 %collective-permute-start.8 = (bf16[2,256,256]{2,1,0:T(8,128)(2,1)S(1)}, bf16[2,256,256]{2,1,0:T(8,128)(2,1)S(1)}, u32[]{:S(2)}, u32[]{:S(2)}) collective-permute-start(bf16[2,256,256]{2,1,0:T(8,128)(2,1)S(1)} %collective-permute-done.5.refs_1_), channel_id=1, source_target_pairs={{0,1},{1,9},{2,3},{3,11},{4,12},{5,4},{6,14},{7,6},{8,0},{9,17},{1... | collective-permute-start | bytes 786440 | tf_op jit(solution)/shard_map/ppermute | solution.py:294
  20.4 6.4 %collective-permute-start.9 = (bf16[2,256,256]{2,1,0:T(8,128)(2,1)S(1)}, bf16[2,256,256]{2,1,0:T(8,128)(2,1)S(1)}, u32[]{:S(2)}, u32[]{:S(2)}) collective-permute-start(bf16[2,256,256]{2,1,0:T(8,128)(2,1)S(1)} %choose.3), channel_id=1, source_target_pairs={{0,2},{1,5},{2,0},{3,7},{4,6},{5,1},{6,4},{7,3},{8,10},{9,13},{10,... | collective-permute-start | bytes 786440 | tf_op jit(solution)/shard_map/ppermute | solution.py:293
  26.4 0.7 %copy-start.2 = (s32[8,2]{0,1:T(2,128)S(1)}, s32[8,2]{0,1:T(2,128)}, u32[]{:S(2)}) copy-start(s32[8,2]{0,1:T(2,128)} %param.6) | copy-start | bytes 196
  28.3 2.0 %collective-permute-start.10 = (bf16[4,272,256]{2,1,0:T(8,128)(2,1)S(1)}, bf16[4,272,256]{2,1,0:T(8,128)(2,1)S(1)}, u32[]{:S(2)}, u32[]{:S(2)}) collective-permute-start(bf16[4,272,256]{2,1,0:T(8,128)(2,1)S(1)} %get-tuple-element.13), channel_id=1, source_target_pairs={{0,1},{1,0},{2,3},{3,2},{4,5},{5,4},{6,7},{7,6},{8,9},{9,8},{10,11... | collective-permute-start | bytes 1671176 | tf_op jit(solution)/shard_map/ppermute | solution.py:312
  28.3 1.9 %copy-start.3 = (s32[4,8,2]{1,2,0:T(2,128)S(1)}, s32[4,8,2]{1,2,0:T(2,128)}, u32[]{:S(2)}) copy-start(s32[4,8,2]{1,2,0:T(2,128)} %param.7) | copy-start | bytes 772
  28.4 1.9 %copy-start.4 = (bf16[768,512]{1,0:T(8,128)(2,1)S(1)}, bf16[768,512]{1,0:T(8,128)(2,1)}, u32[]{:S(2)}) copy-start(bf16[768,512]{1,0:T(8,128)(2,1)} %constant.5.clone.table) | copy-start | bytes 2359300

commit v3 on v2

--- a/solution.py
+++ b/solution.py
@@ -53,16 +53,21 @@
 
 def spectra_of(panels, table):
     count, size, _ = panels.shape
-    first = product(panels.reshape(count * size, size), table[:size, :size]).astype(jnp.bfloat16)
+    right = table[:size, :size]
+    if count > 2:
+        first = [product(panels[k], right).astype(jnp.bfloat16) for k in range(count)]
+    else:
+        stack = product(panels.reshape(count * size, size), right).astype(jnp.bfloat16)
+        first = [stack[k * size : (k + 1) * size] for k in range(count)]
     gauss = table[:size, size:]
-    smooth = [product(gauss, first[k * size : (k + 1) * size]).astype(jnp.bfloat16) for k in range(count)]
-    part = product(jnp.concatenate(smooth, axis=0), table[size : 2 * size]).astype(jnp.bfloat16)
+    smooth = [product(gauss, one).astype(jnp.bfloat16) for one in first]
+    if count > 2:
+        parts = [product(one, table[size : 2 * size]).astype(jnp.bfloat16) for one in smooth]
+    else:
+        stack = product(jnp.concatenate(smooth, axis=0), table[size : 2 * size]).astype(jnp.bfloat16)
+        parts = [stack[k * size : (k + 1) * size] for k in range(count)]
     rows = table[2 * size :]
-    slabs = []
-    for k in range(count):
-        one = part[k * size : (k + 1) * size]
-        slabs.append(product(rows, jnp.concatenate([one[:, :size], one[:, size:]], axis=0)))
-    return slabs
+    return [product(rows, jnp.concatenate([one[:, :size], one[:, size:]], axis=0)) for one in parts]
 
 
 def spectra_kernel(core, *refs):

time: 32.3 us -> 32.1 us (level)
  waiting for transfers between devices: 7.44 us -> 7.82 us
  Pallas kernels: 9.49 us -> 9.12 us
    pallas_call x11, Pallas kernels: 9.49 us -> 9.12 us  [call(): pl.pallas_call(kernel, out_shape=out, in_specs=[first] + [VMEM] * (len(op...]
  transfers between devices with their start and end apart: 11 -> 11, of which waited for: 7 -> 8; matrix products, arithmetic and copies ran while one was open for 0% -> 0% of each run, Pallas kernels for 20% -> 19%
where the time goes in v3:
time: 32.1 us; the launch traced here: 31.9 us
  starting transfers between devices  12 us (37%)
  Pallas kernels  9.12 us (28%)
  waiting for transfers between devices  7.82 us (24%)
  local copies, waits for them, and re-layouts  2.26 us (7%)
  between operations  0.76 us (2%)
    pallas_call x11, Pallas kernels, call(): pl.pallas_call(kernel, out_shape=out, in_specs=[first] + [VMEM] * (len(op...  9.12 us
    ppermute x2, waiting for transfers between devices, shards(): move(after(part, got_swap[0], own), perm=cross_swap)  3.7 us
    ppermute x2, starting transfers between devices, shards(): got_climb = [move(part, perm=climb) for part in got_swap]  3.65 us
    ppermute x2, starting transfers between devices, shards(): got_swap = [move(part, perm=swap) for part in parts]  3.11 us
    ppermute x2, starting transfers between devices, shards(): got_relay = [move(part, perm=relay) for part in picked]  3.11 us
    ppermute x2, waiting for transfers between devices, shards(): got_swap = [move(part, perm=swap) for part in parts]  2.06 us
    ppermute x2, starting transfers between devices, shards(): move(after(part, got_swap[0], own), perm=cross_swap)  2.03 us
    unnamed x10, local copies, waits for them, and re-layouts  1.2 us
  transfers between devices with their start and end apart: 11, of which 8 were waited for; matrix products, arithmetic and copies ran while one was open for 0% of the time, Pallas kernels for 19%

profile of v3, /device:TPU:0, one launch (start us, length us, event | category | flops | bytes accessed | tf_op | source)
XLA Modules:
  0.0 31.9 jit_solution(12141856709248614448)
XLA Ops:
  0.6 1.1 %slice_bitcast_fusion = (bf16[2,256,256]{2,1,0:T(8,128)(2,1)S(1)}, bf16[2,256,256]{2,1,0:T(8,128)(2,1)S(1)}) fusion(bf16[4,1,256,256]{3,2,0,1:T(8,128)(2,1)} %bitcast.10), kind=kLoop, calls=%fused_computation | loop fusion | bytes 1048576 | tf_op jit(solution)/shard_map/slice | solution.py:292
  1.7 3.0 %collective-permute-start = (bf16[2,256,256]{2,1,0:T(8,128)(2,1)S(1)}, bf16[2,256,256]{2,1,0:T(8,128)(2,1)S(1)}, u32[]{:S(2)}, u32[]{:S(2)}) collective-permute-start(bf16[2,256,256]{2,1,0:T(8,128)(2,1)S(1)} %get-tuple-element.9.refs_0_), channel_id=1, source_target_pairs={{0,4},{1,3},{2,6},{3,1},{4,0},{5,7},{6,2},{7,5},{8,12},{9,11},{10,... | collective-permute-start | bytes 786440 | tf_op jit(solution)/shard_map/ppermute | solution.py:293
  4.7 0.1 collective-permute-start.3
  4.8 0.0 copy-start
  4.8 1.1 %copy-done = bf16[784,512]{1,0:T(8,128)(2,1)S(1)} copy-done((bf16[784,512]{1,0:T(8,128)(2,1)S(1)}, bf16[784,512]{1,0:T(8,128)(2,1)}, u32[]{:S(2)}) %copy-start) | copy-done | bytes 802840
  5.9 1.1 %spectra_own.1.refs_0_ = f32[4,272,256]{2,1,0:T(8,128)S(1)} custom-call(bf16[2,256,256]{2,1,0:T(8,128)(2,1)S(1)} %get-tuple-element.9.refs_0_, bf16[2,256,256]{2,1,0:T(8,128)(2,1)S(1)} %get-tuple-element.10.refs_1_, bf16[784,512]{1,0:T(8,128)(2,1)S(1)} %copy-done), custom_call_target="tpu_custom_call" | custom-call | flops 805306368 | bytes 1048576 | tf_op jit(solution)/shard_map/spectra_own/pallas_call | solution.py:251
  7.0 2.1 %collective-permute-done.first.refs_0_ = bf16[2,256,256]{2,1,0:T(8,128)(2,1)S(1)} collective-permute-done((bf16[2,256,256]{2,1,0:T(8,128)(2,1)S(1)}, bf16[2,256,256]{2,1,0:T(8,128)(2,1)S(1)}, u32[]{:S(2)}, u32[]{:S(2)}) %collective-permute-start) | collective-permute-done | bytes 262176 | tf_op jit(solution)/shard_map/ppermute | solution.py:293
  9.1 2.1 %collective-permute-start.1 = (bf16[2,256,256]{2,1,0:T(8,128)(2,1)S(1)}, bf16[2,256,256]{2,1,0:T(8,128)(2,1)S(1)}, u32[]{:S(2)}, u32[]{:S(2)}) collective-permute-start(bf16[2,256,256]{2,1,0:T(8,128)(2,1)S(1)} %collective-permute-done.first.refs_0_), channel_id=1, source_target_pairs={{0,8},{1,0},{2,10},{3,2},{4,5},{5,13},{6,7},{7,15},{8,16},{9,1},{1... | collective-permute-start | bytes 786440 | tf_op jit(solution)/shard_map/ppermute | solution.py:296
  11.2 1.5 %collective-permute-start.4 = (bf16[2,256,256]{2,1,0:T(8,128)(2,1)S(1)}, bf16[2,256,256]{2,1,0:T(8,128)(2,1)S(1)}, u32[]{:S(2)}, u32[]{:S(2)}) collective-permute-start(bf16[2,256,256]{2,1,0:T(8,128)(2,1)S(1)} %get-tuple-element.9.refs_0_), channel_id=1, source_target_pairs={{0,2},{1,5},{2,0},{3,7},{4,6},{5,1},{6,4},{7,3},{8,10},{9,13},{10,... | collective-permute-start | bytes 786440 | tf_op jit(solution)/shard_map/ppermute | solution.py:295
  12.7 0.5 %collective-permute-start.5 = (bf16[2,256,256]{2,1,0:T(8,128)(2,1)S(1)}, bf16[2,256,256]{2,1,0:T(8,128)(2,1)S(1)}, u32[]{:S(2)}, u32[]{:S(2)}) collective-permute-start(bf16[2,256,256]{2,1,0:T(8,128)(2,1)S(1)} %get-tuple-element.10.refs_1_), channel_id=1, source_target_pairs={{0,2},{1,5},{2,0},{3,7},{4,6},{5,1},{6,4},{7,3},{8,10},{9,13},{10,... | collective-permute-start | bytes 786440 | tf_op jit(solution)/shard_map/ppermute | solution.py:295
  13.2 0.0 collective-permute-done.3.refs_1_.first
  13.2 1.6 %collective-permute-start.6 = (bf16[2,256,256]{2,1,0:T(8,128)(2,1)S(1)}, bf16[2,256,256]{2,1,0:T(8,128)(2,1)S(1)}, u32[]{:S(2)}, u32[]{:S(2)}) collective-permute-start(bf16[2,256,256]{2,1,0:T(8,128)(2,1)S(1)} %collective-permute-done.3.refs_1_.first), channel_id=1, source_target_pairs={{0,8},{1,0},{2,10},{3,2},{4,5},{5,13},{6,7},{7,15},{8,16},{9,1},{1... | collective-permute-start | bytes 786440 | tf_op jit(solution)/shard_map/ppermute | solution.py:296
  14.8 0.3 collective-permute-done.1.second.refs_0_
  15.1 0.0 copy-start.1
  15.1 1.6 %collective-permute-start.2 = (bf16[2,256,256]{2,1,0:T(8,128)(2,1)S(1)}, bf16[2,256,256]{2,1,0:T(8,128)(2,1)S(1)}, u32[]{:S(2)}, u32[]{:S(2)}) collective-permute-start(bf16[2,256,256]{2,1,0:T(8,128)(2,1)S(1)} %choose.2), channel_id=1, source_target_pairs={{0,2},{1,5},{2,0},{3,7},{4,6},{5,1},{6,4},{7,3},{8,10},{9,13},{10,... | collective-permute-start | bytes 786440 | tf_op jit(solution)/shard_map/ppermute | solution.py:298
  16.6 0.9 %collective-permute-done.4.refs_0_ = bf16[2,256,256]{2,1,0:T(8,128)(2,1)S(1)} collective-permute-done((bf16[2,256,256]{2,1,0:T(8,128)(2,1)S(1)}, bf16[2,256,256]{2,1,0:T(8,128)(2,1)S(1)}, u32[]{:S(2)}, u32[]{:S(2)}) %collective-permute-start.4) | collective-permute-done | bytes 262176 | tf_op jit(solution)/shard_map/ppermute | solution.py:295
  17.5 0.0 collective-permute-start.7
  17.5 2.8 %collective-permute-done.5.refs_1_ = bf16[2,256,256]{2,1,0:T(8,128)(2,1)S(1)} collective-permute-done((bf16[2,256,256]{2,1,0:T(8,128)(2,1)S(1)}, bf16[2,256,256]{2,1,0:T(8,128)(2,1)S(1)}, u32[]{:S(2)}, u32[]{:S(2)}) %collective-permute-start.5) | collective-permute-done | bytes 262176 | tf_op jit(solution)/shard_map/ppermute | solution.py:295
  20.3 0.0 collective-permute-start.8
  20.3 0.0 collective-permute-done.6.refs_1_.second
  20.4 1.6 %collective-permute-start.9 = (bf16[2,256,256]{2,1,0:T(8,128)(2,1)S(1)}, bf16[2,256,256]{2,1,0:T(8,128)(2,1)S(1)}, u32[]{:S(2)}, u32[]{:S(2)}) collective-permute-start(bf16[2,256,256]{2,1,0:T(8,128)(2,1)S(1)} %choose.3), channel_id=1, source_target_pairs={{0,2},{1,5},{2,0},{3,7},{4,6},{5,1},{6,4},{7,3},{8,10},{9,13},{10,... | collective-permute-start | bytes 786440 | tf_op jit(solution)/shard_map/ppermute | solution.py:298
  21.9 0.0 copy-done.1
  21.9 1.1 %spectra_cross.1.refs_2_ = f32[4,272,256]{2,1,0:T(8,128)S(1)} custom-call(bf16[2,256,256]{2,1,0:T(8,128)(2,1)S(1)} %collective-permute-done.4.refs_0_, bf16[2,256,256]{2,1,0:T(8,128)(2,1)S(1)} %collective-permute-done.5.refs_1_, bf16[784,512]{1,0:T(8,128)(2,1)S(1)} %copy-done.1), custom_call_target="tpu_custom_call" | custom-call | flops 1000000 | bytes 1048576 | tf_op jit(solution)/shard_map/spectra_cross/pallas_call | solution.py:251
  23.0 0.1 collective-permute-done.2.refs_0_
  23.1 1.1 %spectra_swap.1.refs_1_ = f32[4,272,256]{2,1,0:T(8,128)S(1)} custom-call(bf16[2,256,256]{2,1,0:T(8,128)(2,1)S(1)} %collective-permute-done.first.refs_0_, bf16[2,256,256]{2,1,0:T(8,128)(2,1)S(1)} %collective-permute-done.3.refs_1_.first, bf16[784,512]{1,0:T(8,128)(2,1)S(1)} %copy-done.1), custom_call_target="tpu_custom_call" | custom-call | flops 805306368 | bytes 1048576 | tf_op jit(solution)/shard_map/spectra_swap/pallas_call | solution.py:251
  24.2 1.1 %spectra_climb.1.refs_3_ = f32[4,272,256]{2,1,0:T(8,128)S(1)} custom-call(bf16[2,256,256]{2,1,0:T(8,128)(2,1)S(1)} %collective-permute-done.1.second.refs_0_, bf16[2,256,256]{2,1,0:T(8,128)(2,1)S(1)} %collective-permute-done.6.refs_1_.second, bf16[784,512]{1,0:T(8,128)(2,1)S(1)} %copy-done.1), custom_call_target="tpu_custom_call" | custom-call | flops 1000000 | bytes 1048576 | tf_op jit(solution)/shard_map/spectra_climb/pallas_call | solution.py:251
  25.3 0.8 %spectra_relay.1.refs_5_ = f32[2,272,256]{2,1,0:T(8,128)S(1)} custom-call(bf16[2,256,256]{2,1,0:T(8,128)(2,1)S(1)} %collective-permute-done.2.refs_0_, bf16[784,512]{1,0:T(8,128)(2,1)S(1)} %copy-done.1), custom_call_target="tpu_custom_call" | custom-call | flops 800000000 | bytes 1048576 | tf_op jit(solution)/shard_map/spectra_relay/pallas_call | solution.py:251
  26.2 0.0 copy-start.2
  26.2 0.0 collective-permute-done.7.refs_0_
  26.2 0.5 %collective-permute-done.8.refs_1_ = bf16[2,256,256]{2,1,0:T(8,128)(2,1)S(1)} collective-permute-done((bf16[2,256,256]{2,1,0:T(8,128)(2,1)S(1)}, bf16[2,256,256]{2,1,0:T(8,128)(2,1)S(1)}, u32[]{:S(2)}, u32[]{:S(2)}) %collective-permute-start.8) | collective-permute-done | bytes 262176 | tf_op jit(solution)/shard_map/ppermute | solution.py:299
  26.7 0.1 collective-permute-done.9.refs_6_
  26.8 0.0 copy-done.2
  26.8 1.2 %cross_other.1 = (bf16[4,272,256]{2,1,0:T(8,128)(2,1)S(1)}, f32[2,272,256]{2,1,0:T(8,128)S(1)}) custom-call(s32[2,8]{1,0:T(2,128)S(1)} %bitcast.7, f32[4,272,256]{2,1,0:T(8,128)S(1)} %spectra_own.1.refs_0_, f32[4,272,256]{2,1,0:T(8,128)S(1)} %spectra_swap.1.refs_1_, f32[4,272,256]{2,1,0:T(8,128)S(1)} %spectra_cross.1.refs_2_, ...), custom_call_target="tpu_custom_call" | custom-call | flops 536870912 | bytes 1048576 | tf_op jit(solution)/shard_map/cross_other/pallas_call | solution.py:251
  28.1 0.1 collective-permute-start.10
  28.2 0.0 copy-start.3
  28.2 0.0 copy-start.4
  28.2 0.9 %cross_mine.1.mine = bf16[4,272,256]{2,1,0:T(8,128)(2,1)S(1)} custom-call(s32[2,8]{1,0:T(2,128)S(1)} %bitcast.8, f32[4,272,256]{2,1,0:T(8,128)S(1)} %spectra_own.1.refs_0_, f32[4,272,256]{2,1,0:T(8,128)S(1)} %spectra_swap.1.refs_1_, f32[4,272,256]{2,1,0:T(8,128)S(1)} %spectra_cross.1.refs_2_, f32[4,272,256]{2,1,0:T(8,128)S(1)} %spectra_climb.1.refs_3_, ...), custom_call_target="tpu_custom_call" | custom-call | flops 33554432 | bytes 1048576 | tf_op jit(solution)/shard_map/cross_mine/pallas_call | solution.py:251
  29.1 1.0 %collective-permute-done.10.other = bf16[4,272,256]{2,1,0:T(8,128)(2,1)S(1)} collective-permute-done((bf16[4,272,256]{2,1,0:T(8,128)(2,1)S(1)}, bf16[4,272,256]{2,1,0:T(8,128)(2,1)S(1)}, u32[]{:S(2)}, u32[]{:S(2)}) %collective-permute-start.10) | collective-permute-done | bytes 557088 | tf_op jit(solution)/shard_map/ppermute | solution.py:317
  30.1 0.0 copy-done.3
  30.1 0.0 copy-done.4
  30.1 1.8 %surface.1 = (bf16[4,256,256]{2,1,0:T(8,128)(2,1)}, f32[4,8]{1,0:T(4,128)}) custom-call(s32[4,2,8]{2,1,0:T(2,128)S(1)} %bitcast.9, bf16[4,272,256]{2,1,0:T(8,128)(2,1)S(1)} %cross_mine.1.mine, bf16[4,272,256]{2,1,0:T(8,128)(2,1)S(1)} %collective-permute-done.10.other, bf16[768,512]{1,0:T(8,128)(2,1)S(1)} %copy-done.4), custom_call_target="tpu_custom_call" | custom-call | flops 1073741824 | bytes 1048576 | tf_op jit(solution)/shard_map/surface/pallas_call | solution.py:251
  (3 shorter events, 0.0 us)
Async XLA Ops:
  1.7 7.4 %collective-permute-start = (bf16[2,256,256]{2,1,0:T(8,128)(2,1)S(1)}, bf16[2,256,256]{2,1,0:T(8,128)(2,1)S(1)}, u32[]{:S(2)}, u32[]{:S(2)}) collective-permute-start(bf16[2,256,256]{2,1,0:T(8,128)(2,1)S(1)} %get-tuple-element.9.refs_0_), channel_id=1, source_target_pairs={{0,4},{1,3},{2,6},{3,1},{4,0},{5,7},{6,2},{7,5},{8,12},{9,11},{10,... | collective-permute-start | bytes 786440 | tf_op jit(solution)/shard_map/ppermute | solution.py:293
  4.7 8.5 %collective-permute-start.3 = (bf16[2,256,256]{2,1,0:T(8,128)(2,1)S(1)}, bf16[2,256,256]{2,1,0:T(8,128)(2,1)S(1)}, u32[]{:S(2)}, u32[]{:S(2)}) collective-permute-start(bf16[2,256,256]{2,1,0:T(8,128)(2,1)S(1)} %get-tuple-element.10.refs_1_), channel_id=1, source_target_pairs={{0,4},{1,3},{2,6},{3,1},{4,0},{5,7},{6,2},{7,5},{8,12},{9,11},{10,... | collective-permute-start | bytes 786440 | tf_op jit(solution)/shard_map/ppermute | solution.py:293
  4.8 1.1 %copy-start = (bf16[784,512]{1,0:T(8,128)(2,1)S(1)}, bf16[784,512]{1,0:T(8,128)(2,1)}, u32[]{:S(2)}) copy-start(bf16[784,512]{1,0:T(8,128)(2,1)} %constant.4.clone.refs_2_.refs_1_.refs_7_) | copy-start | bytes 2408452
  9.1 6.0 %collective-permute-start.1 = (bf16[2,256,256]{2,1,0:T(8,128)(2,1)S(1)}, bf16[2,256,256]{2,1,0:T(8,128)(2,1)S(1)}, u32[]{:S(2)}, u32[]{:S(2)}) collective-permute-start(bf16[2,256,256]{2,1,0:T(8,128)(2,1)S(1)} %collective-permute-done.first.refs_0_), channel_id=1, source_target_pairs={{0,8},{1,0},{2,10},{3,2},{4,5},{5,13},{6,7},{7,15},{8,16},{9,1},{1... | collective-permute-start | bytes 786440 | tf_op jit(solution)/shard_map/ppermute | solution.py:296
  11.2 6.4 %collective-permute-start.4 = (bf16[2,256,256]{2,1,0:T(8,128)(2,1)S(1)}, bf16[2,256,256]{2,1,0:T(8,128)(2,1)S(1)}, u32[]{:S(2)}, u32[]{:S(2)}) collective-permute-start(bf16[2,256,256]{2,1,0:T(8,128)(2,1)S(1)} %get-tuple-element.9.refs_0_), channel_id=1, source_target_pairs={{0,2},{1,5},{2,0},{3,7},{4,6},{5,1},{6,4},{7,3},{8,10},{9,13},{10,... | collective-permute-start | bytes 786440 | tf_op jit(solution)/shard_map/ppermute | solution.py:295
  12.7 7.7 %collective-permute-start.5 = (bf16[2,256,256]{2,1,0:T(8,128)(2,1)S(1)}, bf16[2,256,256]{2,1,0:T(8,128)(2,1)S(1)}, u32[]{:S(2)}, u32[]{:S(2)}) collective-permute-start(bf16[2,256,256]{2,1,0:T(8,128)(2,1)S(1)} %get-tuple-element.10.refs_1_), channel_id=1, source_target_pairs={{0,2},{1,5},{2,0},{3,7},{4,6},{5,1},{6,4},{7,3},{8,10},{9,13},{10,... | collective-permute-start | bytes 786440 | tf_op jit(solution)/shard_map/ppermute | solution.py:295
  13.2 7.2 %collective-permute-start.6 = (bf16[2,256,256]{2,1,0:T(8,128)(2,1)S(1)}, bf16[2,256,256]{2,1,0:T(8,128)(2,1)S(1)}, u32[]{:S(2)}, u32[]{:S(2)}) collective-permute-start(bf16[2,256,256]{2,1,0:T(8,128)(2,1)S(1)} %collective-permute-done.3.refs_1_.first), channel_id=1, source_target_pairs={{0,8},{1,0},{2,10},{3,2},{4,5},{5,13},{6,7},{7,15},{8,16},{9,1},{1... | collective-permute-start | bytes 786440 | tf_op jit(solution)/shard_map/ppermute | solution.py:296
  15.1 6.9 %copy-start.1 = (bf16[784,512]{1,0:T(8,128)(2,1)S(1)}, bf16[784,512]{1,0:T(8,128)(2,1)}, u32[]{:S(2)}) copy-start(bf16[784,512]{1,0:T(8,128)(2,1)} %constant.4.clone.refs_2_.refs_1_.refs_7_) | copy-start | bytes 2408452
  15.1 8.1 %collective-permute-start.2 = (bf16[2,256,256]{2,1,0:T(8,128)(2,1)S(1)}, bf16[2,256,256]{2,1,0:T(8,128)(2,1)S(1)}, u32[]{:S(2)}, u32[]{:S(2)}) collective-permute-start(bf16[2,256,256]{2,1,0:T(8,128)(2,1)S(1)} %choose.2), channel_id=1, source_target_pairs={{0,2},{1,5},{2,0},{3,7},{4,6},{5,1},{6,4},{7,3},{8,10},{9,13},{10,... | collective-permute-start | bytes 786440 | tf_op jit(solution)/shard_map/ppermute | solution.py:298
  17.5 8.6 %collective-permute-start.7 = (bf16[2,256,256]{2,1,0:T(8,128)(2,1)S(1)}, bf16[2,256,256]{2,1,0:T(8,128)(2,1)S(1)}, u32[]{:S(2)}, u32[]{:S(2)}) collective-permute-start(bf16[2,256,256]{2,1,0:T(8,128)(2,1)S(1)} %collective-permute-done.4.refs_0_), channel_id=1, source_target_pairs={{0,1},{1,9},{2,3},{3,11},{4,12},{5,4},{6,14},{7,6},{8,0},{9,17},{1... | collective-permute-start | bytes 786440 | tf_op jit(solution)/shard_map/ppermute | solution.py:299
  20.3 6.4 %collective-permute-start.8 = (bf16[2,256,256]{2,1,0:T(8,128)(2,1)S(1)}, bf16[2,256,256]{2,1,0:T(8,128)(2,1)S(1)}, u32[]{:S(2)}, u32[]{:S(2)}) collective-permute-start(bf16[2,256,256]{2,1,0:T(8,128)(2,1)S(1)} %collective-permute-done.5.refs_1_), channel_id=1, source_target_pairs={{0,1},{1,9},{2,3},{3,11},{4,12},{5,4},{6,14},{7,6},{8,0},{9,17},{1... | collective-permute-start | bytes 786440 | tf_op jit(solution)/shard_map/ppermute | solution.py:299
  20.4 6.4 %collective-permute-start.9 = (bf16[2,256,256]{2,1,0:T(8,128)(2,1)S(1)}, bf16[2,256,256]{2,1,0:T(8,128)(2,1)S(1)}, u32[]{:S(2)}, u32[]{:S(2)}) collective-permute-start(bf16[2,256,256]{2,1,0:T(8,128)(2,1)S(1)} %choose.3), channel_id=1, source_target_pairs={{0,2},{1,5},{2,0},{3,7},{4,6},{5,1},{6,4},{7,3},{8,10},{9,13},{10,... | collective-permute-start | bytes 786440 | tf_op jit(solution)/shard_map/ppermute | solution.py:298
  26.2 0.7 %copy-start.2 = (s32[8,2]{0,1:T(2,128)S(1)}, s32[8,2]{0,1:T(2,128)}, u32[]{:S(2)}) copy-start(s32[8,2]{0,1:T(2,128)} %param.6) | copy-start | bytes 196
  28.1 2.0 %collective-permute-start.10 = (bf16[4,272,256]{2,1,0:T(8,128)(2,1)S(1)}, bf16[4,272,256]{2,1,0:T(8,128)(2,1)S(1)}, u32[]{:S(2)}, u32[]{:S(2)}) collective-permute-start(bf16[4,272,256]{2,1,0:T(8,128)(2,1)S(1)} %get-tuple-element.13), channel_id=1, source_target_pairs={{0,1},{1,0},{2,3},{3,2},{4,5},{5,4},{6,7},{7,6},{8,9},{9,8},{10,11... | collective-permute-start | bytes 1671176 | tf_op jit(solution)/shard_map/ppermute | solution.py:317
  28.2 1.9 %copy-start.3 = (s32[4,8,2]{1,2,0:T(2,128)S(1)}, s32[4,8,2]{1,2,0:T(2,128)}, u32[]{:S(2)}) copy-start(s32[4,8,2]{1,2,0:T(2,128)} %param.7) | copy-start | bytes 772
  28.2 1.9 %copy-start.4 = (bf16[768,512]{1,0:T(8,128)(2,1)S(1)}, bf16[768,512]{1,0:T(8,128)(2,1)}, u32[]{:S(2)}) copy-start(bf16[768,512]{1,0:T(8,128)(2,1)} %constant.5.clone.table) | copy-start | bytes 2359300

commit v4 on v3

--- a/solution.py
+++ b/solution.py
@@ -289,7 +289,7 @@
     half = tile_dev // 2
 
     spectra = functools.partial(spectra_calls, forward, slab)
-    parts = (local[:half], local[half:])
+    parts = (local[:half], lax.optimization_barrier(local)[half:])
     got_swap = [move(part, perm=swap) for part in parts]
     own = spectra("own", None, *parts)
     got_cross = [move(after(part, got_swap[0], own), perm=cross_swap) for part in parts]

time: 32.1 us -> 32.1 us (level)
  waiting for transfers between devices: 7.82 us -> 6.84 us
  local copies, waits for them, and re-layouts: 2.26 us -> 3.13 us
    ppermute x2, waiting for transfers between devices: 2.06 us -> 1.09 us  [shards(): got_swap = [move(part, perm=swap) for part in parts]]
    slice x1 -> x2, local copies, waits for them, and re-layouts: 1.07 us -> 1.94 us  [shards(): parts = (local[:half], lax.optimization_barrier(local)[half:])]
  transfers between devices with their start and end apart: 11 -> 11, of which waited for: 8 -> 8; matrix products, arithmetic and copies ran while one was open for 0% -> 3% of each run, Pallas kernels for 19% -> 19%
where the time goes in v4:
time: 32.1 us; the launch traced here: 31.8 us
  starting transfers between devices  12 us (37%)
  Pallas kernels  9.12 us (28%)
  waiting for transfers between devices  6.84 us (21%)
  local copies, waits for them, and re-layouts  3.13 us (10%)
  between operations  0.77 us (2%)
    pallas_call x11, Pallas kernels, call(): pl.pallas_call(kernel, out_shape=out, in_specs=[first] + [VMEM] * (len(op...  9.12 us
    ppermute x2, waiting for transfers between devices, shards(): move(after(part, got_swap[0], own), perm=cross_swap)  3.7 us
    ppermute x2, starting transfers between devices, shards(): got_climb = [move(part, perm=climb) for part in got_swap]  3.65 us
    ppermute x2, starting transfers between devices, shards(): got_swap = [move(part, perm=swap) for part in parts]  3.11 us
    ppermute x2, starting transfers between devices, shards(): got_relay = [move(part, perm=relay) for part in picked]  3.11 us
    ppermute x2, starting transfers between devices, shards(): move(after(part, got_swap[0], own), perm=cross_swap)  2.03 us
    slice x2, local copies, waits for them, and re-layouts, shards(): parts = (local[:half], lax.optimization_barrier(local)[half:])  1.94 us
    unnamed x10, local copies, waits for them, and re-layouts  1.2 us
  transfers between devices with their start and end apart: 11, of which 8 were waited for; matrix products, arithmetic and copies ran while one was open for 3% of the time, Pallas kernels for 19%

profile of v4, /device:TPU:0, one launch (start us, length us, event | category | flops | bytes accessed | tf_op | source)
XLA Modules:
  0.0 31.8 jit_solution(14967817028673082991)
XLA Ops:
  0.6 1.0 %slice_bitcast_fusion.refs_0_ = bf16[2,256,256]{2,1,0:T(8,128)(2,1)S(1)} fusion(bf16[4,1,256,256]{3,2,0,1:T(8,128)(2,1)} %bitcast.9), kind=kLoop, calls=%fused_computation | loop fusion | bytes 524288 | tf_op jit(solution)/shard_map/slice | solution.py:292
  1.6 3.0 %collective-permute-start = (bf16[2,256,256]{2,1,0:T(8,128)(2,1)S(1)}, bf16[2,256,256]{2,1,0:T(8,128)(2,1)S(1)}, u32[]{:S(2)}, u32[]{:S(2)}) collective-permute-start(bf16[2,256,256]{2,1,0:T(8,128)(2,1)S(1)} %slice_bitcast_fusion.refs_0_), channel_id=1, source_target_pairs={{0,4},{1,3},{2,6},{3,1},{4,0},{5,7},{6,2},{7,5},{8,12},{9,11},{10,... | collective-permute-start | bytes 786440 | tf_op jit(solution)/shard_map/ppermute | solution.py:293
  4.6 1.0 %slice.13.refs_1_ = bf16[2,256,256]{2,1,0:T(8,128)(2,1)S(1)} slice(bf16[4,256,256]{2,1,0:T(8,128)(2,1)} %bitcast.10), slice={[2:4], [0:256], [0:256]} | slice | bytes 524288 | tf_op jit(solution)/shard_map/slice | solution.py:292
  5.6 0.1 collective-permute-start.3
  5.7 0.0 copy-start
  5.7 1.1 %copy-done = bf16[784,512]{1,0:T(8,128)(2,1)S(1)} copy-done((bf16[784,512]{1,0:T(8,128)(2,1)S(1)}, bf16[784,512]{1,0:T(8,128)(2,1)}, u32[]{:S(2)}) %copy-start) | copy-done | bytes 802840
  6.8 1.1 %spectra_own.1.refs_0_ = f32[4,272,256]{2,1,0:T(8,128)S(1)} custom-call(bf16[2,256,256]{2,1,0:T(8,128)(2,1)S(1)} %slice_bitcast_fusion.refs_0_, bf16[2,256,256]{2,1,0:T(8,128)(2,1)S(1)} %slice.13.refs_1_, bf16[784,512]{1,0:T(8,128)(2,1)S(1)} %copy-done), custom_call_target="tpu_custom_call" | custom-call | flops 805306368 | bytes 1048576 | tf_op jit(solution)/shard_map/spectra_own/pallas_call | solution.py:251
  7.9 1.1 %collective-permute-done.first.refs_0_ = bf16[2,256,256]{2,1,0:T(8,128)(2,1)S(1)} collective-permute-done((bf16[2,256,256]{2,1,0:T(8,128)(2,1)S(1)}, bf16[2,256,256]{2,1,0:T(8,128)(2,1)S(1)}, u32[]{:S(2)}, u32[]{:S(2)}) %collective-permute-start) | collective-permute-done | bytes 262176 | tf_op jit(solution)/shard_map/ppermute | solution.py:293
  9.0 2.1 %collective-permute-start.1 = (bf16[2,256,256]{2,1,0:T(8,128)(2,1)S(1)}, bf16[2,256,256]{2,1,0:T(8,128)(2,1)S(1)}, u32[]{:S(2)}, u32[]{:S(2)}) collective-permute-start(bf16[2,256,256]{2,1,0:T(8,128)(2,1)S(1)} %collective-permute-done.first.refs_0_), channel_id=1, source_target_pairs={{0,8},{1,0},{2,10},{3,2},{4,5},{5,13},{6,7},{7,15},{8,16},{9,1},{1... | collective-permute-start | bytes 786440 | tf_op jit(solution)/shard_map/ppermute | solution.py:296
  11.1 1.5 %collective-permute-start.4 = (bf16[2,256,256]{2,1,0:T(8,128)(2,1)S(1)}, bf16[2,256,256]{2,1,0:T(8,128)(2,1)S(1)}, u32[]{:S(2)}, u32[]{:S(2)}) collective-permute-start(bf16[2,256,256]{2,1,0:T(8,128)(2,1)S(1)} %slice_bitcast_fusion.refs_0_), channel_id=1, source_target_pairs={{0,2},{1,5},{2,0},{3,7},{4,6},{5,1},{6,4},{7,3},{8,10},{9,13},{10,... | collective-permute-start | bytes 786440 | tf_op jit(solution)/shard_map/ppermute | solution.py:295
  12.6 0.5 %collective-permute-start.5 = (bf16[2,256,256]{2,1,0:T(8,128)(2,1)S(1)}, bf16[2,256,256]{2,1,0:T(8,128)(2,1)S(1)}, u32[]{:S(2)}, u32[]{:S(2)}) collective-permute-start(bf16[2,256,256]{2,1,0:T(8,128)(2,1)S(1)} %slice.13.refs_1_), channel_id=1, source_target_pairs={{0,2},{1,5},{2,0},{3,7},{4,6},{5,1},{6,4},{7,3},{8,10},{9,13},{10,... | collective-permute-start | bytes 786440 | tf_op jit(solution)/shard_map/ppermute | solution.py:295
  13.1 0.0 collective-permute-done.3.refs_1_.first
  13.1 1.6 %collective-permute-start.6 = (bf16[2,256,256]{2,1,0:T(8,128)(2,1)S(1)}, bf16[2,256,256]{2,1,0:T(8,128)(2,1)S(1)}, u32[]{:S(2)}, u32[]{:S(2)}) collective-permute-start(bf16[2,256,256]{2,1,0:T(8,128)(2,1)S(1)} %collective-permute-done.3.refs_1_.first), channel_id=1, source_target_pairs={{0,8},{1,0},{2,10},{3,2},{4,5},{5,13},{6,7},{7,15},{8,16},{9,1},{1... | collective-permute-start | bytes 786440 | tf_op jit(solution)/shard_map/ppermute | solution.py:296
  14.7 0.3 collective-permute-done.1.second.refs_0_
  15.0 0.0 copy-start.1
  15.0 1.6 %collective-permute-start.2 = (bf16[2,256,256]{2,1,0:T(8,128)(2,1)S(1)}, bf16[2,256,256]{2,1,0:T(8,128)(2,1)S(1)}, u32[]{:S(2)}, u32[]{:S(2)}) collective-permute-start(bf16[2,256,256]{2,1,0:T(8,128)(2,1)S(1)} %choose.2), channel_id=1, source_target_pairs={{0,2},{1,5},{2,0},{3,7},{4,6},{5,1},{6,4},{7,3},{8,10},{9,13},{10,... | collective-permute-start | bytes 786440 | tf_op jit(solution)/shard_map/ppermute | solution.py:298
  16.5 0.9 %collective-permute-done.4.refs_0_ = bf16[2,256,256]{2,1,0:T(8,128)(2,1)S(1)} collective-permute-done((bf16[2,256,256]{2,1,0:T(8,128)(2,1)S(1)}, bf16[2,256,256]{2,1,0:T(8,128)(2,1)S(1)}, u32[]{:S(2)}, u32[]{:S(2)}) %collective-permute-start.4) | collective-permute-done | bytes 262176 | tf_op jit(solution)/shard_map/ppermute | solution.py:295
  17.4 0.0 collective-permute-start.7
  17.4 2.8 %collective-permute-done.5.refs_1_ = bf16[2,256,256]{2,1,0:T(8,128)(2,1)S(1)} collective-permute-done((bf16[2,256,256]{2,1,0:T(8,128)(2,1)S(1)}, bf16[2,256,256]{2,1,0:T(8,128)(2,1)S(1)}, u32[]{:S(2)}, u32[]{:S(2)}) %collective-permute-start.5) | collective-permute-done | bytes 262176 | tf_op jit(solution)/shard_map/ppermute | solution.py:295
  20.2 0.0 collective-permute-start.8
  20.2 0.0 collective-permute-done.6.refs_1_.second
  20.3 1.6 %collective-permute-start.9 = (bf16[2,256,256]{2,1,0:T(8,128)(2,1)S(1)}, bf16[2,256,256]{2,1,0:T(8,128)(2,1)S(1)}, u32[]{:S(2)}, u32[]{:S(2)}) collective-permute-start(bf16[2,256,256]{2,1,0:T(8,128)(2,1)S(1)} %choose.3), channel_id=1, source_target_pairs={{0,2},{1,5},{2,0},{3,7},{4,6},{5,1},{6,4},{7,3},{8,10},{9,13},{10,... | collective-permute-start | bytes 786440 | tf_op jit(solution)/shard_map/ppermute | solution.py:298
  21.8 0.0 copy-done.1
  21.8 1.1 %spectra_cross.1.refs_2_ = f32[4,272,256]{2,1,0:T(8,128)S(1)} custom-call(bf16[2,256,256]{2,1,0:T(8,128)(2,1)S(1)} %collective-permute-done.4.refs_0_, bf16[2,256,256]{2,1,0:T(8,128)(2,1)S(1)} %collective-permute-done.5.refs_1_, bf16[784,512]{1,0:T(8,128)(2,1)S(1)} %copy-done.1), custom_call_target="tpu_custom_call" | custom-call | flops 1000000 | bytes 1048576 | tf_op jit(solution)/shard_map/spectra_cross/pallas_call | solution.py:251
  22.9 0.1 collective-permute-done.2.refs_0_
  23.1 1.1 %spectra_swap.1.refs_1_ = f32[4,272,256]{2,1,0:T(8,128)S(1)} custom-call(bf16[2,256,256]{2,1,0:T(8,128)(2,1)S(1)} %collective-permute-done.first.refs_0_, bf16[2,256,256]{2,1,0:T(8,128)(2,1)S(1)} %collective-permute-done.3.refs_1_.first, bf16[784,512]{1,0:T(8,128)(2,1)S(1)} %copy-done.1), custom_call_target="tpu_custom_call" | custom-call | flops 805306368 | bytes 1048576 | tf_op jit(solution)/shard_map/spectra_swap/pallas_call | solution.py:251
  24.1 1.1 %spectra_climb.1.refs_3_ = f32[4,272,256]{2,1,0:T(8,128)S(1)} custom-call(bf16[2,256,256]{2,1,0:T(8,128)(2,1)S(1)} %collective-permute-done.1.second.refs_0_, bf16[2,256,256]{2,1,0:T(8,128)(2,1)S(1)} %collective-permute-done.6.refs_1_.second, bf16[784,512]{1,0:T(8,128)(2,1)S(1)} %copy-done.1), custom_call_target="tpu_custom_call" | custom-call | flops 1000000 | bytes 1048576 | tf_op jit(solution)/shard_map/spectra_climb/pallas_call | solution.py:251
  25.2 0.8 %spectra_relay.1.refs_5_ = f32[2,272,256]{2,1,0:T(8,128)S(1)} custom-call(bf16[2,256,256]{2,1,0:T(8,128)(2,1)S(1)} %collective-permute-done.2.refs_0_, bf16[784,512]{1,0:T(8,128)(2,1)S(1)} %copy-done.1), custom_call_target="tpu_custom_call" | custom-call | flops 800000000 | bytes 1048576 | tf_op jit(solution)/shard_map/spectra_relay/pallas_call | solution.py:251
  26.1 0.0 copy-start.2
  26.1 0.0 collective-permute-done.7.refs_0_
  26.1 0.5 %collective-permute-done.8.refs_1_ = bf16[2,256,256]{2,1,0:T(8,128)(2,1)S(1)} collective-permute-done((bf16[2,256,256]{2,1,0:T(8,128)(2,1)S(1)}, bf16[2,256,256]{2,1,0:T(8,128)(2,1)S(1)}, u32[]{:S(2)}, u32[]{:S(2)}) %collective-permute-start.8) | collective-permute-done | bytes 262176 | tf_op jit(solution)/shard_map/ppermute | solution.py:299
  26.6 0.1 collective-permute-done.9.refs_6_
  26.7 0.0 copy-done.2
  26.8 1.2 %cross_other.1 = (bf16[4,272,256]{2,1,0:T(8,128)(2,1)S(1)}, f32[2,272,256]{2,1,0:T(8,128)S(1)}) custom-call(s32[2,8]{1,0:T(2,128)S(1)} %bitcast.6, f32[4,272,256]{2,1,0:T(8,128)S(1)} %spectra_own.1.refs_0_, f32[4,272,256]{2,1,0:T(8,128)S(1)} %spectra_swap.1.refs_1_, f32[4,272,256]{2,1,0:T(8,128)S(1)} %spectra_cross.1.refs_2_, ...), custom_call_target="tpu_custom_call" | custom-call | flops 536870912 | bytes 1048576 | tf_op jit(solution)/shard_map/cross_other/pallas_call | solution.py:251
  28.0 0.1 collective-permute-start.10
  28.1 0.0 copy-start.3
  28.1 0.0 copy-start.4
  28.1 0.9 %cross_mine.1.mine = bf16[4,272,256]{2,1,0:T(8,128)(2,1)S(1)} custom-call(s32[2,8]{1,0:T(2,128)S(1)} %bitcast.7, f32[4,272,256]{2,1,0:T(8,128)S(1)} %spectra_own.1.refs_0_, f32[4,272,256]{2,1,0:T(8,128)S(1)} %spectra_swap.1.refs_1_, f32[4,272,256]{2,1,0:T(8,128)S(1)} %spectra_cross.1.refs_2_, f32[4,272,256]{2,1,0:T(8,128)S(1)} %spectra_climb.1.refs_3_, ...), custom_call_target="tpu_custom_call" | custom-call | flops 33554432 | bytes 1048576 | tf_op jit(solution)/shard_map/cross_mine/pallas_call | solution.py:251
  29.0 1.0 %collective-permute-done.10.other = bf16[4,272,256]{2,1,0:T(8,128)(2,1)S(1)} collective-permute-done((bf16[4,272,256]{2,1,0:T(8,128)(2,1)S(1)}, bf16[4,272,256]{2,1,0:T(8,128)(2,1)S(1)}, u32[]{:S(2)}, u32[]{:S(2)}) %collective-permute-start.10) | collective-permute-done | bytes 557088 | tf_op jit(solution)/shard_map/ppermute | solution.py:317
  30.0 0.0 copy-done.3
  30.0 0.0 copy-done.4
  30.0 1.8 %surface.1 = (bf16[4,256,256]{2,1,0:T(8,128)(2,1)}, f32[4,8]{1,0:T(4,128)}) custom-call(s32[4,2,8]{2,1,0:T(2,128)S(1)} %bitcast.8, bf16[4,272,256]{2,1,0:T(8,128)(2,1)S(1)} %cross_mine.1.mine, bf16[4,272,256]{2,1,0:T(8,128)(2,1)S(1)} %collective-permute-done.10.other, bf16[768,512]{1,0:T(8,128)(2,1)S(1)} %copy-done.4), custom_call_target="tpu_custom_call" | custom-call | flops 1073741824 | bytes 1048576 | tf_op jit(solution)/shard_map/surface/pallas_call | solution.py:251
  (3 shorter events, 0.0 us)
Async XLA Ops:
  1.6 7.4 %collective-permute-start = (bf16[2,256,256]{2,1,0:T(8,128)(2,1)S(1)}, bf16[2,256,256]{2,1,0:T(8,128)(2,1)S(1)}, u32[]{:S(2)}, u32[]{:S(2)}) collective-permute-start(bf16[2,256,256]{2,1,0:T(8,128)(2,1)S(1)} %slice_bitcast_fusion.refs_0_), channel_id=1, source_target_pairs={{0,4},{1,3},{2,6},{3,1},{4,0},{5,7},{6,2},{7,5},{8,12},{9,11},{10,... | collective-permute-start | bytes 786440 | tf_op jit(solution)/shard_map/ppermute | solution.py:293
  5.6 7.5 %collective-permute-start.3 = (bf16[2,256,256]{2,1,0:T(8,128)(2,1)S(1)}, bf16[2,256,256]{2,1,0:T(8,128)(2,1)S(1)}, u32[]{:S(2)}, u32[]{:S(2)}) collective-permute-start(bf16[2,256,256]{2,1,0:T(8,128)(2,1)S(1)} %slice.13.refs_1_), channel_id=1, source_target_pairs={{0,4},{1,3},{2,6},{3,1},{4,0},{5,7},{6,2},{7,5},{8,12},{9,11},{10,... | collective-permute-start | bytes 786440 | tf_op jit(solution)/shard_map/ppermute | solution.py:293
  5.7 1.1 %copy-start = (bf16[784,512]{1,0:T(8,128)(2,1)S(1)}, bf16[784,512]{1,0:T(8,128)(2,1)}, u32[]{:S(2)}) copy-start(bf16[784,512]{1,0:T(8,128)(2,1)} %constant.4.clone.refs_2_.refs_1_.refs_7_) | copy-start | bytes 2408452
  9.0 6.0 %collective-permute-start.1 = (bf16[2,256,256]{2,1,0:T(8,128)(2,1)S(1)}, bf16[2,256,256]{2,1,0:T(8,128)(2,1)S(1)}, u32[]{:S(2)}, u32[]{:S(2)}) collective-permute-start(bf16[2,256,256]{2,1,0:T(8,128)(2,1)S(1)} %collective-permute-done.first.refs_0_), channel_id=1, source_target_pairs={{0,8},{1,0},{2,10},{3,2},{4,5},{5,13},{6,7},{7,15},{8,16},{9,1},{1... | collective-permute-start | bytes 786440 | tf_op jit(solution)/shard_map/ppermute | solution.py:296
  11.1 6.4 %collective-permute-start.4 = (bf16[2,256,256]{2,1,0:T(8,128)(2,1)S(1)}, bf16[2,256,256]{2,1,0:T(8,128)(2,1)S(1)}, u32[]{:S(2)}, u32[]{:S(2)}) collective-permute-start(bf16[2,256,256]{2,1,0:T(8,128)(2,1)S(1)} %slice_bitcast_fusion.refs_0_), channel_id=1, source_target_pairs={{0,2},{1,5},{2,0},{3,7},{4,6},{5,1},{6,4},{7,3},{8,10},{9,13},{10,... | collective-permute-start | bytes 786440 | tf_op jit(solution)/shard_map/ppermute | solution.py:295
  12.6 7.7 %collective-permute-start.5 = (bf16[2,256,256]{2,1,0:T(8,128)(2,1)S(1)}, bf16[2,256,256]{2,1,0:T(8,128)(2,1)S(1)}, u32[]{:S(2)}, u32[]{:S(2)}) collective-permute-start(bf16[2,256,256]{2,1,0:T(8,128)(2,1)S(1)} %slice.13.refs_1_), channel_id=1, source_target_pairs={{0,2},{1,5},{2,0},{3,7},{4,6},{5,1},{6,4},{7,3},{8,10},{9,13},{10,... | collective-permute-start | bytes 786440 | tf_op jit(solution)/shard_map/ppermute | solution.py:295
  13.1 7.2 %collective-permute-start.6 = (bf16[2,256,256]{2,1,0:T(8,128)(2,1)S(1)}, bf16[2,256,256]{2,1,0:T(8,128)(2,1)S(1)}, u32[]{:S(2)}, u32[]{:S(2)}) collective-permute-start(bf16[2,256,256]{2,1,0:T(8,128)(2,1)S(1)} %collective-permute-done.3.refs_1_.first), channel_id=1, source_target_pairs={{0,8},{1,0},{2,10},{3,2},{4,5},{5,13},{6,7},{7,15},{8,16},{9,1},{1... | collective-permute-start | bytes 786440 | tf_op jit(solution)/shard_map/ppermute | solution.py:296
  15.0 6.9 %copy-start.1 = (bf16[784,512]{1,0:T(8,128)(2,1)S(1)}, bf16[784,512]{1,0:T(8,128)(2,1)}, u32[]{:S(2)}) copy-start(bf16[784,512]{1,0:T(8,128)(2,1)} %constant.4.clone.refs_2_.refs_1_.refs_7_) | copy-start | bytes 2408452
  15.0 8.1 %collective-permute-start.2 = (bf16[2,256,256]{2,1,0:T(8,128)(2,1)S(1)}, bf16[2,256,256]{2,1,0:T(8,128)(2,1)S(1)}, u32[]{:S(2)}, u32[]{:S(2)}) collective-permute-start(bf16[2,256,256]{2,1,0:T(8,128)(2,1)S(1)} %choose.2), channel_id=1, source_target_pairs={{0,2},{1,5},{2,0},{3,7},{4,6},{5,1},{6,4},{7,3},{8,10},{9,13},{10,... | collective-permute-start | bytes 786440 | tf_op jit(solution)/shard_map/ppermute | solution.py:298
  17.4 8.7 %collective-permute-start.7 = (bf16[2,256,256]{2,1,0:T(8,128)(2,1)S(1)}, bf16[2,256,256]{2,1,0:T(8,128)(2,1)S(1)}, u32[]{:S(2)}, u32[]{:S(2)}) collective-permute-start(bf16[2,256,256]{2,1,0:T(8,128)(2,1)S(1)} %collective-permute-done.4.refs_0_), channel_id=1, source_target_pairs={{0,1},{1,9},{2,3},{3,11},{4,12},{5,4},{6,14},{7,6},{8,0},{9,17},{1... | collective-permute-start | bytes 786440 | tf_op jit(solution)/shard_map/ppermute | solution.py:299
  20.2 6.4 %collective-permute-start.8 = (bf16[2,256,256]{2,1,0:T(8,128)(2,1)S(1)}, bf16[2,256,256]{2,1,0:T(8,128)(2,1)S(1)}, u32[]{:S(2)}, u32[]{:S(2)}) collective-permute-start(bf16[2,256,256]{2,1,0:T(8,128)(2,1)S(1)} %collective-permute-done.5.refs_1_), channel_id=1, source_target_pairs={{0,1},{1,9},{2,3},{3,11},{4,12},{5,4},{6,14},{7,6},{8,0},{9,17},{1... | collective-permute-start | bytes 786440 | tf_op jit(solution)/shard_map/ppermute | solution.py:299
  20.3 6.4 %collective-permute-start.9 = (bf16[2,256,256]{2,1,0:T(8,128)(2,1)S(1)}, bf16[2,256,256]{2,1,0:T(8,128)(2,1)S(1)}, u32[]{:S(2)}, u32[]{:S(2)}) collective-permute-start(bf16[2,256,256]{2,1,0:T(8,128)(2,1)S(1)} %choose.3), channel_id=1, source_target_pairs={{0,2},{1,5},{2,0},{3,7},{4,6},{5,1},{6,4},{7,3},{8,10},{9,13},{10,... | collective-permute-start | bytes 786440 | tf_op jit(solution)/shard_map/ppermute | solution.py:298
  26.1 0.7 %copy-start.2 = (s32[8,2]{0,1:T(2,128)S(1)}, s32[8,2]{0,1:T(2,128)}, u32[]{:S(2)}) copy-start(s32[8,2]{0,1:T(2,128)} %param.6) | copy-start | bytes 196
  28.0 2.0 %collective-permute-start.10 = (bf16[4,272,256]{2,1,0:T(8,128)(2,1)S(1)}, bf16[4,272,256]{2,1,0:T(8,128)(2,1)S(1)}, u32[]{:S(2)}, u32[]{:S(2)}) collective-permute-start(bf16[4,272,256]{2,1,0:T(8,128)(2,1)S(1)} %get-tuple-element.13), channel_id=1, source_target_pairs={{0,1},{1,0},{2,3},{3,2},{4,5},{5,4},{6,7},{7,6},{8,9},{9,8},{10,11... | collective-permute-start | bytes 1671176 | tf_op jit(solution)/shard_map/ppermute | solution.py:317
  28.1 1.9 %copy-start.3 = (s32[4,8,2]{1,2,0:T(2,128)S(1)}, s32[4,8,2]{1,2,0:T(2,128)}, u32[]{:S(2)}) copy-start(s32[4,8,2]{1,2,0:T(2,128)} %param.7) | copy-start | bytes 772
  28.1 1.9 %copy-start.4 = (bf16[768,512]{1,0:T(8,128)(2,1)S(1)}, bf16[768,512]{1,0:T(8,128)(2,1)}, u32[]{:S(2)}) copy-start(bf16[768,512]{1,0:T(8,128)(2,1)} %constant.5.clone.table) | copy-start | bytes 2359300
